TPU v7x, 32 devices: a whole 2x2x4 slice. The times are simulated.
32 devices in a mesh: cent: 8 (over z, y), grp: 4 (over x, core).
Axes of the slice: x: 2, y: 2, z: 4, core: 2. Of those that a mesh axis runs over, the one named last changes fastest.
Arguments:
- queries: bfloat16 [64, 32, 128], P('grp'), may hold values from -6 to 6
- centroids: bfloat16 [262144, 128], P('cent'), may hold values from -0.5 to 0.5
- candidates: int32 [4, 8, 2, 64], P('grp', 'cent'), may hold values from 0 to 16383, as said below
- token_codes: int32 [16384, 128], P(('cent', 'grp')), may hold values from 0 to 32767
- resid_words: int32 [16384, 32, 128], P(('cent', 'grp')), may hold values from 0 to 255
- lengths: int32 [16384], P(('cent', 'grp')), may hold values from 1 to 128
- levels: float32 [4, 128], replicated, may hold values from -0.3125 to 0.3125
Outputs:
- token_best: float32 [64, 32], P('grp')
- passage_scores: float32 [4, 8, 2, 64], P('grp', 'cent')
Inputs may be any that keep to these rules, and one draw needn't show every extreme that they name: `candidates`: the entries of one [g, c] block are all different and name at most 8 passages of any one owner block (passages owner * 512 to owner * 512 + 511); one owner block gets exactly 8 from every [g, c] block.
All inputs are finite; a program needn't handle non-finite values.
Results may differ from a plain program's by a relative error of at most 0.0003.
Values may be sent and summed in bfloat16 or wider, within the bound.
No kernel may reach another device: no remote copies, remote signals or barrier semaphores. Data moves between devices by JAX's collectives and lax.ppermute only.
A program may use at most 128 MiB of HBM per device.

v0:
```python
import jax
import jax.numpy as jnp
from jax import lax
from jax.sharding import PartitionSpec as P


def unpack_levels(words, levels):
    fields = []
    for shift_index in range(4):
        fields.append(jnp.right_shift(words, 2 * shift_index))
    stacked = jnp.stack(fields, axis=2)
    level_codes = stacked.reshape(words.shape[0], words.shape[1] * 4, words.shape[2])
    low_bit = jnp.bitwise_and(level_codes, 1) == 1
    high_bit = jnp.bitwise_and(level_codes, 2) == 2
    lower_pair = jnp.where(low_bit, levels[1], levels[0])
    upper_pair = jnp.where(low_bit, levels[3], levels[2])
    return jnp.where(high_bit, upper_pair, lower_pair)


def dequantize(centroid_rows, words, levels):
    dequantized = centroid_rows.astype(jnp.float32) + unpack_levels(words, levels)
    inverse_norm = lax.rsqrt(jnp.sum(dequantized * dequantized, axis=-1, keepdims=True) + 1e-06)
    return (dequantized * inverse_norm).astype(jnp.bfloat16)


def maxsim_rows(query_blocks, passages, passage_lengths):
    scores = jnp.einsum("sqd,spd->sqp", query_blocks, passages, preferred_element_type=jnp.float32)
    position = lax.broadcasted_iota(jnp.int32, scores.shape, 2)
    inside = position < passage_lengths[:, None, None]
    return jnp.max(jnp.where(inside, scores, -1000000000.0), axis=2)


def slot_table(cand_row, pass_dev):
    owners = cand_row // pass_dev
    row_count = cand_row.shape[0]
    earlier_pair = lax.broadcasted_iota(
        jnp.int32, (row_count, row_count), 0
    ) > lax.broadcasted_iota(jnp.int32, (row_count, row_count), 1)
    same_owner = owners[:, None] == owners[None, :]
    slot_of = jnp.sum(jnp.where(same_owner & earlier_pair, 1, 0), axis=1).astype(jnp.int32)
    return (owners, slot_of)


def send_buffer(own_queries, cand_row, target, slot_total, cand_count, pass_dev):
    slot_grid = jnp.arange(slot_total, dtype=jnp.int32)
    pair_grid = jnp.arange(cand_row.shape[0], dtype=jnp.int32)
    matches = slot_grid[:, None] == target[None, :]
    picked = jnp.sum(jnp.where(matches, pair_grid[None, :], 0), axis=1)
    send_blocks = jnp.take(own_queries, picked // cand_count, axis=0)
    send_ids = jnp.take(cand_row, picked) % pass_dev
    return (send_blocks, send_ids)


def shards(queries, centroids, candidates, token_codes, resid_words, lengths, levels):
    group_rows, query_len, feature_width = queries.shape
    cent_dev = centroids.shape[0]
    pass_dev = token_codes.shape[0]
    plen_slots = token_codes.shape[1]
    per_device = candidates.shape[2]
    cand_count = candidates.shape[3]
    pair_count = per_device * cand_count
    cent_count = lax.axis_size("cent")
    group_count = lax.axis_size("grp")
    devices = cent_count * group_count
    capacity = max(2, 2 * pair_count // devices)
    cent_index = lax.axis_index("cent")
    own_queries = lax.dynamic_slice_in_dim(queries, cent_index * per_device, per_device, 0)
    cand_row = candidates.reshape(pair_count)
    owners, slot_of = slot_table(cand_row, pass_dev)
    target = owners * capacity + slot_of
    send_blocks, send_ids = send_buffer(
        own_queries, cand_row, target, devices * capacity, cand_count, pass_dev
    )
    blocks = lax.all_to_all(
        send_blocks.reshape(devices, capacity, query_len, feature_width),
        ("cent", "grp"),
        split_axis=0,
        concat_axis=0,
        tiled=True,
    )
    passage_ids = lax.all_to_all(
        send_ids.reshape(devices, capacity),
        ("cent", "grp"),
        split_axis=0,
        concat_axis=0,
        tiled=True,
    )
    sources, item_count = passage_ids.shape
    flat_ids = passage_ids.reshape(sources * item_count)
    code_rows = jnp.take(token_codes, flat_ids, axis=0)
    flat_codes = code_rows.reshape(sources * item_count * plen_slots)
    centroid_rows = jnp.take(centroids, flat_codes, axis=0).reshape(
        sources * item_count, plen_slots, feature_width
    )
    word_rows = jnp.take(resid_words, flat_ids, axis=0)
    embedded = dequantize(centroid_rows, word_rows, levels)
    flat_blocks = blocks.reshape(sources * item_count, query_len, feature_width)
    maxima = maxsim_rows(flat_blocks, embedded, jnp.take(lengths, flat_ids))
    rows_out = maxima.reshape(sources, item_count, query_len)
    flat_queries = queries.reshape(group_rows * query_len, feature_width)
    block_size = min(cent_dev, 2048)

    def block_step(block_index, running_best):
        centroid_block = lax.dynamic_slice_in_dim(
            centroids, block_index * block_size, block_size, 0
        )
        scores = lax.dot_general(
            flat_queries,
            centroid_block,
            (((1,), (1,)), ((), ())),
            preferred_element_type=jnp.float32,
        )
        return jnp.maximum(running_best, jnp.max(scores, axis=1))

    initial = jnp.full((group_rows * query_len,), -jnp.inf, jnp.float32)
    local_best = lax.fori_loop(0, cent_dev // block_size, block_step, initial)
    token_best = lax.pmax(local_best, "cent").reshape(group_rows, query_len)
    returned = lax.all_to_all(rows_out, ("cent", "grp"), split_axis=0, concat_axis=0, tiled=True)
    pair_rows = jnp.take(returned.reshape(devices * capacity, query_len), target, axis=0)
    totals = jnp.sum(pair_rows, axis=1) / query_len
    passage_scores = totals.reshape(1, 1, per_device, cand_count)
    return (token_best, passage_scores)


def solution(mesh):
    placed = (
        P("grp", None, None),
        P("cent", None),
        P("grp", "cent", None, None),
        P(("cent", "grp"), None),
        P(("cent", "grp"), None, None),
        P(("cent", "grp")),
        P(),
    )
    return jax.shard_map(
        shards,
        mesh=mesh,
        in_specs=placed,
        out_specs=(P("grp", None), P("grp", "cent", None, None)),
        check_vma=False,
    )
```

profile of v0, /device:TPU:0, one launch (start us, length us, event | category | flops | bytes accessed | tf_op | source)
XLA Modules:
  0.0 311.8 jit_solution(11695244557551122314)
XLA Ops:
  1.9 1.9 gather_fusion
  4.5 7.3 %all-to-all-start = ((s32[32,1,8]{2,1,0:T(1,128)}), s32[32,1,8]{2,1,0:T(1,128)S(1)}, u32[]{:S(2)}, u32[]{:S(2)}) async-start(s32[32,1,8]{2,1,0:T(1,128)} %bitcast.3), calls=%async_computation | async-start | bytes 32768 | tf_op jit(solution)/shard_map/all_to_all | solution.py:81
  14.2 29.2 %while.14 = (s32[]{:T(128)}, f32[512]{0:T(512)S(1)}, bf16[32768,128]{1,0:T(8,128)(2,1)}, bf16[512,128]{1,0:T(8,128)(2,1)}, s32[]{:T(128)}, /*index=5*/s32[]{:T(128)}, s32[]{:T(128)}, s32[]{:T(128)}) while((s32[]{:T(128)}, f32[512]{0:T(512)S(1)}, bf16[32768,128]{1,0:T(8,128)(2,1)}, bf16[512,128]{1,0:T(8,128)(2,1)}, s32[]{:T(128)}, ...), condition=%wide.region_2.3_spmd.clone, body=%wide.region_0.2_spmd.clone.sunk | while | flops 269484544 | bytes 663697 | solution.py:116
  14.2 1.8 convolution_reduce_fusion.2
  16.1 1.8 convolution_reduce_fusion.2
  17.9 1.8 convolution_reduce_fusion.2
  19.7 1.8 convolution_reduce_fusion.2
  21.6 1.8 convolution_reduce_fusion.2
  23.4 1.8 convolution_reduce_fusion.2
  25.2 1.8 convolution_reduce_fusion.2
  27.1 1.8 convolution_reduce_fusion.2
  28.9 1.8 convolution_reduce_fusion.2
  30.7 1.8 convolution_reduce_fusion.2
  38.0 1.8 convolution_reduce_fusion.2
  46.2 22.5 %pmax.7 = f32[16,32]{1,0:T(8,128)} all-reduce(f32[16,32]{1,0:T(8,128)S(1)} %reshape.554), channel_id=1, replica_groups=mesh['cent'=8,'grp'=4] {'cent'}, use_global_device_ids=true, to_apply=%region_3.4 | all-reduce | flops 512 | bytes 4096 | tf_op jit(solution)/shard_map/pmax | solution.py:117
  68.7 2.7 all-to-all-start.1
  72.8 1.9 gather_fusion.1
  74.8 6.1 %gather_fusion.5 = s32[256,32,128]{2,1,0:T(8,128)} fusion(s32[512,32,128]{2,1,0:T(8,128)} %param.13, s32[1024]{0:T(1024)S(1)} %pad_clamp_fusion.2), kind=kCustom, calls=%fused_computation.5 | custom fusion | bytes 8389632 | tf_op jit(solution)/shard_map/jit(_take)/gather | solution.py:95
  81.9 3.2 %fusion.7 = (s32[256,32,1,128]{3,1,0,2:T(8,128)S(1)}, s32[256,32,1,128]{3,1,0,2:T(8,128)S(1)}, s32[256,32,1,128]{3,1,0,2:T(8,128)S(1)}, s32[256,32,1,128]{3,1,0,2:T(8,128)S(1)}) fusion(s32[256,32,128]{2,1,0:T(8,128)} %gather_fusion.5, pred[256]{0:T(512)(128)(4,1)S(1)} %get-tuple-element.110), kind=kLoop, calls=%fused_computation.25 | loop fusion | flops 5242880 | bytes 20971776 | tf_op jit(solution)/shard_map/shift_right_arithmetic | solution.py:10
  85.1 7.5 %and_compare_fusion.1 = (pred[256,32,4,128]{3,1,0,2:T(8,128)(4,1)}, pred[256,32,4,128]{3,1,0,2:T(8,128)(4,1)S(1)}) fusion(s32[256,32,1,128]{3,1,0,2:T(8,128)S(1)} %get-tuple-element.116, s32[256,32,1,128]{3,1,0,2:T(8,128)S(1)} %get-tuple-element.115, s32[256,32,1,128]{3,1,0,2:T(8,128)S(1)} %get-tuple-element.114, s32[256,32,1,128]{3,1,0,2:T(8,128)S(1)} %get-tuple-element.113), kind=kLoop, calls=%fused_computation.15 | loop fusion | flops 29360128 | bytes 25165824 | tf_op jit(solution)/shard_map/eq | solution.py:14
  92.6 18.2 %copy.46 = pred[256,32,4,128]{3,2,1,0:T(4,128)(4,1)} copy(pred[256,32,4,128]{3,1,0,2:T(8,128)(4,1)} %get-tuple-element.111) | data formatting | bytes 8388608 | tf_op jit(solution)/shard_map/eq | solution.py:14
  110.8 14.6 %copy.47 = pred[256,32,4,128]{3,2,1,0:T(4,128)(4,1)} copy(pred[256,32,4,128]{3,1,0,2:T(8,128)(4,1)S(1)} %get-tuple-element.112) | data formatting | bytes 8388608 | tf_op jit(solution)/shard_map/eq | solution.py:13
  125.6 113.9 %gather_fusion.4 = bf16[32768,128]{1,0:T(8,128)(2,1)} fusion(bf16[32768,128]{1,0:T(8,128)(2,1)} %get-tuple-element.172, s32[32768]{0:T(1024)S(1)} %broadcast_clamp_fusion), kind=kCustom, calls=%fused_computation.4 | custom fusion | bytes 16908288 | tf_op jit(solution)/shard_map/jit(_take)/gather | solution.py:92
  239.6 3.6 %copy.45 = pred[256,32,4]{2,1,0:T(8,128)(4,1)S(1)} copy(pred[256,32,4]{0,2,1:T(4,128)(4,1)S(1)} %compare_and_fusion) | data formatting | bytes 65536 | tf_op jit(solution)/shard_map/jit(_take)/and | solution.py:92
  243.2 4.0 %broadcast_in_dim.153 = pred[32768]{0:T(1024)(128)(4,1)S(1)} reshape(pred[256,32,4]{2,1,0:T(8,128)(4,1)S(1)} %copy.45) | data formatting | bytes 65536 | tf_op jit(solution)/shard_map/jit(_take)/broadcast_in_dim | solution.py:92
  247.2 13.3 %multiply_reduce_fusion = f32[32768]{0:T(1024)S(1)} fusion(pred[32768,128]{1,0:T(8,128)(4,1)} %bitcast.53, pred[32768,128]{1,0:T(8,128)(4,1)} %bitcast.54, f32[128]{0:T(128)S(1)} %get-tuple-element.119, f32[128]{0:T(128)S(1)} %get-tuple-element.120, f32[128]{0:T(128)S(1)} %get-tuple-element.118, f32[128]{0:T(128)S(1)} %get-tuple-element.117, ...), kind=kLoop, calls=%fused_computation.13 | loop fusion | flops 33521664 | bytes 16943104 | tf_op jit(solution)/shard_map/reduce_sum | solution.py:22
  260.5 4.4 %copy.42 = pred[256,32,4,128]{3,0,2,1:T(8,128)(4,1)} copy(pred[256,32,4,128]{3,1,0,2:T(8,128)(4,1)S(1)} %copy-done.5) | data formatting | bytes 8388608 | tf_op jit(solution)/shard_map/eq | solution.py:14
  264.9 4.4 %copy.43 = pred[256,32,4,128]{3,0,2,1:T(8,128)(4,1)} copy(pred[256,32,4,128]{3,1,0,2:T(8,128)(4,1)S(1)} %copy-done.4) | data formatting | bytes 8388608 | tf_op jit(solution)/shard_map/eq | solution.py:13
  269.6 14.1 %multiply_convert_fusion = bf16[256,128,128]{2,0,1:T(8,128)(2,1)} fusion(pred[256,32,4,128]{3,0,2,1:T(8,128)(4,1)} %copy.43, pred[256,32,4,128]{3,0,2,1:T(8,128)(4,1)} %copy.42, bf16[256,128,128]{2,1,0:T(8,128)(2,1)} %bitcast.52, f32[256,128]{0,1:T(8,128)S(1)} %copy.48, f32[128]{0:T(128)S(1)} %get-tuple-element.119, f32[128]{0:T(128)S(1)} %get-tuple-element.120, ...), kind=kLoop, calls=%fused_computation.12 | loop fusion | flops 33554432 | bytes 25331712 | tf_op jit(solution)/shard_map/convert_element_type | solution.py:23
  283.7 11.0 %select_reduce_fusion = f32[256,32]{1,0:T(8,128)S(1)} fusion(s32[256]{0:T(256)S(1)} %get-tuple-element.109, bf16[256,32,128]{2,1,0:T(8,128)(2,1)S(1)} %bitcast.57, bf16[256,128,128]{2,0,1:T(8,128)(2,1)} %multiply_convert_fusion), kind=kOutput, calls=%fused_computation.20 | convolution fusion | flops 271572992 | bytes 10519552 | tf_op jit(solution)/shard_map/sqd,spd->sqp/dot_general | solution.py:27
  295.4 5.8 %all-to-all-start.2 = ((f32[32,1,256]{2,1,0:T(1,128)}), f32[32,1,256]{2,1,0:T(1,128)S(1)}, u32[]{:S(2)}, u32[]{:S(2)}) async-start(f32[32,1,256]{2,1,0:T(1,128)} %reshape.630), calls=%async_computation.2 | async-start | bytes 65536 | tf_op jit(solution)/shard_map/all_to_all | solution.py:118
  301.3 7.2 %all-to-all-done.2 = f32[32,1,256]{2,1,0:T(1,128)S(1)} async-done(((f32[32,1,256]{2,1,0:T(1,128)}), f32[32,1,256]{2,1,0:T(1,128)S(1)}, u32[]{:S(2)}, u32[]{:S(2)}) %all-to-all-start.2) | async-done | bytes 32800 | tf_op jit(solution)/shard_map/all_to_all | solution.py:118
  (82 shorter events, 22.6 us)
Async XLA Ops:
  0.6 80.3 %copy-start = (s32[512,128]{1,0:T(8,128)S(1)}, s32[512,128]{1,0:T(8,128)}, u32[]{:S(2)}) copy-start(s32[512,128]{1,0:T(8,128)} %param.12) | copy-start | bytes 786436
  4.5 64.2 %all-to-all-start = ((s32[32,1,8]{2,1,0:T(1,128)}), s32[32,1,8]{2,1,0:T(1,128)S(1)}, u32[]{:S(2)}, u32[]{:S(2)}) async-start(s32[32,1,8]{2,1,0:T(1,128)} %bitcast.3), calls=%async_computation | async-start | bytes 32768 | tf_op jit(solution)/shard_map/all_to_all | solution.py:81
  14.2 58.6 %copy-start.2 = (s32[512]{0:T(512)S(1)}, s32[512]{0:T(512)}, u32[]{:S(2)}) copy-start(s32[512]{0:T(512)} %param.14) | copy-start | bytes 6148
  68.7 215.0 %all-to-all-start.1 = ((bf16[32,8,32,128]{3,2,1,0:T(8,128)(2,1)}), bf16[32,8,32,128]{3,2,1,0:T(8,128)(2,1)S(1)}, u32[]{:S(2)}, u32[]{:S(2)}) async-start(bf16[32,8,32,128]{3,2,1,0:T(8,128)(2,1)} %broadcast_select_fusion), calls=%async_computation.1 | async-start | bytes 4194304 | tf_op jit(solution)/shard_map/all_to_all | solution.py:74
  92.6 32.8 %copy-start.3 = (pred[256,32,4,128]{3,1,0,2:T(8,128)(4,1)}, pred[256,32,4,128]{3,1,0,2:T(8,128)(4,1)S(1)}, u32[]{:S(2)}) copy-start(pred[256,32,4,128]{3,1,0,2:T(8,128)(4,1)S(1)} %get-tuple-element.112) | copy-start | bytes 12582916
  247.2 13.3 %copy-start.5 = (pred[256,32,4,128]{3,1,0,2:T(8,128)(4,1)S(1)}, pred[256,32,4,128]{3,1,0,2:T(8,128)(4,1)}, u32[]{:S(2)}) copy-start(pred[256,32,4,128]{3,1,0,2:T(8,128)(4,1)} %get-tuple-element.111) | copy-start | bytes 12582916
  260.5 4.4 %copy-start.4 = (pred[256,32,4,128]{3,1,0,2:T(8,128)(4,1)S(1)}, pred[256,32,4,128]{3,1,0,2:T(8,128)(4,1)}, u32[]{:S(2)}) copy-start(pred[256,32,4,128]{3,1,0,2:T(8,128)(4,1)} %copy-done.3) | copy-start | bytes 12582916
  269.5 41.8 %copy-start.1 = (s32[512,128]{1,0:T(8,128)S(1)}, s32[512,128]{1,0:T(8,128)}, u32[]{:S(2)}) copy-start(s32[512,128]{1,0:T(8,128)} %param.12) | copy-start | bytes 786436
  295.4 13.1 %all-to-all-start.2 = ((f32[32,1,256]{2,1,0:T(1,128)}), f32[32,1,256]{2,1,0:T(1,128)S(1)}, u32[]{:S(2)}, u32[]{:S(2)}) async-start(f32[32,1,256]{2,1,0:T(1,128)} %reshape.630), calls=%async_computation.2 | async-start | bytes 65536 | tf_op jit(solution)/shard_map/all_to_all | solution.py:118
where the time goes:
time: 317 us; the launch traced here: 312 us
  local copies, waits for them, and re-layouts  182 us (57%)
  other arithmetic  42.9 us (14%)
  matrix products  39.6 us (12%)
  blocking collectives  22.5 us (7%)
  starting transfers between devices  15.9 us (5%)
  waiting for transfers between devices  7.24 us (2%)
    gather x1, local copies, waits for them, and re-layouts, shards(): jnp.take(centroids, flat_codes, axis=0)  114 us
    dot_general x16, matrix products, block_step(): lax.dot_general(flat_queries, centroid_block, (((1,), (1,)), ((), ())), p...  28.5 us
    eq x2, local copies, waits for them, and re-layouts, unpack_levels(): high_bit = jnp.bitwise_and(level_codes, 2) == 2  22.6 us
    pmax x1, blocking collectives, shards(): token_best = lax.pmax(local_best, 'cent').reshape(group_rows, query_len)  22.5 us
    eq x2, local copies, waits for them, and re-layouts, unpack_levels(): low_bit = jnp.bitwise_and(level_codes, 1) == 1  19 us
    convert_element_type x1, other arithmetic, dequantize(): return (dequantized * inverse_norm).astype(jnp.bfloat16)  14.1 us
    reduce_sum x1, other arithmetic, dequantize(): jnp.sum(dequantized * dequantized, axis=-1, keepdims=True) + 1e-06  13.3 us
    dot_general x1, matrix products, maxsim_rows(): jnp.einsum('sqd,spd->sqp', query_blocks, passages, preferred_element_type...  11 us
  transfers between devices with their start and end apart: 3, of which 1 were waited for; matrix products, arithmetic and copies ran while one was open for 79% of the time, Pallas kernels for 0%

commit v1 on v0

v1 whole, which is shorter than its diff:
```python
import functools

import jax
import jax.numpy as jnp
from jax import lax
from jax.experimental import pallas as pl
from jax.experimental.pallas import tpu as pltpu
from jax.sharding import PartitionSpec as P

MASKED = -1000000000.0
LANES = 128
SUB = 8
FIELDS = 4
BLOCKS = 8
MIB = 1 << 20


def transposed_by_eye(row):
    size = row.shape[1]
    down = lax.broadcasted_iota(jnp.int32, (size, size), 0)
    across = lax.broadcasted_iota(jnp.int32, (size, size), 1)
    return jnp.sum(jnp.where(down == across, row, 0.0), axis=1, keepdims=True)


def best_kernel(owner_shift, capacity, q_ref, cand_ref, cent_ref, best_ref, target_ref, qt_ref, acc_ref):
    step = pl.program_id(0)
    rows = 512

    @pl.when(step == 0)
    def _():
        qt_ref[...] = jnp.transpose(q_ref[...].astype(jnp.float32)).astype(jnp.bfloat16)
        acc_ref[...] = jnp.full(acc_ref.shape, -jnp.inf, jnp.float32)
        owners = jnp.right_shift(cand_ref[...], owner_shift).astype(jnp.float32)
        pairs = owners.shape[1]
        earlier = lax.broadcasted_iota(jnp.int32, (pairs, pairs), 0) < lax.broadcasted_iota(
            jnp.int32, (pairs, pairs), 1
        )
        same = transposed_by_eye(owners) == owners
        slots = jnp.sum(jnp.where(same & earlier, 1.0, 0.0), axis=0, keepdims=True)
        target_ref[...] = (owners * capacity + slots).astype(jnp.int32)

    def tile(index, best):
        block = cent_ref[pl.ds(pl.multiple_of(index * rows, rows), rows), :]
        scores = jnp.dot(block, qt_ref[...], preferred_element_type=jnp.float32)
        return jnp.maximum(best, jnp.max(scores.reshape(rows // SUB, SUB, scores.shape[1]), axis=0))

    acc_ref[...] = lax.fori_loop(0, cent_ref.shape[0] // rows, tile, acc_ref[...])

    @pl.when(step == pl.num_programs(0) - 1)
    def _():
        best = jnp.max(acc_ref[...], axis=0, keepdims=True)
        width = best_ref.shape[1]
        for index in range(best_ref.shape[0]):
            best_ref[index : index + 1, :] = best[:, index * width : (index + 1) * width]


def centroid_best(queries, cand_row, centroids, pass_dev, capacity):
    group_rows, query_len, width = queries.shape
    tokens = group_rows * query_len
    cent_dev = centroids.shape[0]
    block = min(cent_dev, 4096)
    pairs = cand_row.shape[1]
    return pl.pallas_call(
        functools.partial(best_kernel, pass_dev.bit_length() - 1, capacity),
        grid=(cent_dev // block,),
        in_specs=[
            pl.BlockSpec((tokens, width), lambda i: (0, 0)),
            pl.BlockSpec((1, pairs), lambda i: (0, 0)),
            pl.BlockSpec((block, width), lambda i: (i, 0)),
        ],
        out_specs=[
            pl.BlockSpec((group_rows, query_len), lambda i: (0, 0)),
            pl.BlockSpec((1, pairs), lambda i: (0, 0)),
        ],
        out_shape=[
            jax.ShapeDtypeStruct((group_rows, query_len), jnp.float32),
            jax.ShapeDtypeStruct((1, pairs), jnp.int32),
        ],
        scratch_shapes=[
            pltpu.VMEM((width, tokens), jnp.bfloat16),
            pltpu.VMEM((SUB, tokens), jnp.float32),
        ],
        compiler_params=pltpu.CompilerParams(vmem_limit_bytes=24 * MIB),
        cost_estimate=pl.CostEstimate(
            flops=2 * tokens * cent_dev * width, bytes_accessed=2 * cent_dev * width, transcendentals=0
        ),
        name="centroid_best",
    )(queries.reshape(tokens, width), cand_row, centroids)


def score_kernel(
    sizes,
    me_ref,
    cand_ref,
    levels_ref,
    query_ref,
    cent_hbm,
    words_hbm,
    codes_hbm,
    lens_hbm,
    out_ref,
    staged,
    table,
    words,
    query_t,
    embed,
    maxima,
    ids_vmem,
    ids,
    codes,
    lens,
    work,
    work_quad,
    item_pass,
    item_len,
    item_lane,
    table_sem,
    words_sem,
    small_sem,
):
    group_count, cent_count, per_device, query_len, capacity, pass_dev, cand_count = sizes
    sources, pairs = cand_ref.shape
    items = sources * capacity
    tiles = words.shape[1] // SUB
    tile_tokens = SUB * FIELDS
    quad_sources = LANES // (per_device * query_len)
    quads = sources // quad_sources
    per_bits = per_device.bit_length() - 1
    tile_bits = tiles.bit_length() - 1
    parts = table_sem.shape[0]
    part_rows = staged.shape[0] // parts
    word_parts = words_sem.shape[0]
    part_pass = pass_dev // word_parts

    def table_copy(part):
        rows = pl.ds(part * part_rows, part_rows)
        return pltpu.make_async_copy(cent_hbm.at[rows, :], staged.at[rows, :], table_sem.at[part])

    def words_copy(part):
        rows = pl.ds(part * part_pass, part_pass)
        return pltpu.make_async_copy(words_hbm.at[rows], words.at[rows], words_sem.at[part])

    lens_copy = pltpu.make_async_copy(lens_hbm, lens, small_sem.at[0])
    codes_copy = pltpu.make_async_copy(codes_hbm, codes, small_sem.at[1])
    lens_copy.start()
    for part in range(parts):
        table_copy(part).start()
    codes_copy.start()
    for part in range(word_parts):
        words_copy(part).start()

    first = me_ref[0] * pass_dev
    local = cand_ref[...] - first
    mine = (local >= 0) & (local < pass_dev)
    earlier = lax.broadcasted_iota(jnp.int32, (pairs, pairs), 0) < lax.broadcasted_iota(
        jnp.int32, (pairs, pairs), 1
    )
    slots = jnp.dot(
        mine.astype(jnp.bfloat16), earlier.astype(jnp.bfloat16), preferred_element_type=jnp.float32
    )
    which = lax.broadcasted_iota(jnp.int32, local.shape, 1) >= cand_count
    tagged = (local * per_device + which.astype(jnp.int32) + 1).astype(jnp.float32)
    lane = lax.broadcasted_iota(jnp.int32, ids_vmem.shape, 1)
    found = jnp.zeros(ids_vmem.shape, jnp.float32)
    for slot in range(capacity):
        chosen = jnp.sum(jnp.where(mine & (slots == slot), tagged, 0.0), axis=1, keepdims=True)
        found = jnp.where(lane == slot, chosen, found)
    ids_vmem[...] = found.astype(jnp.int32)
    ids_copy = pltpu.make_async_copy(ids_vmem, ids, small_sem.at[2])
    ids_copy.start()

    def turn(quad, carry):
        block = query_ref[pl.ds(pl.multiple_of(quad * LANES, LANES), LANES), :]
        query_t[quad] = jnp.transpose(block.astype(jnp.float32)).astype(jnp.bfloat16)
        return carry

    lax.fori_loop(0, quads, turn, 0)
    maxima[...] = jnp.full(maxima.shape, MASKED, jnp.float32)
    embed[...] = jnp.zeros(embed.shape, embed.dtype)
    lens_copy.wait()
    ids_copy.wait()

    item_pass[items] = 0
    item_len[items] = 0
    item_lane[items] = -1
    spare = items * tiles

    def fill(quad, count):
        start = count
        group = quad // (cent_count // quad_sources)
        cent = (quad % (cent_count // quad_sources)) * quad_sources
        for part in range(quad_sources):
            source = (cent + part) * group_count + group
            for slot in range(capacity):
                tag = ids[source, slot] - 1
                item = source * capacity + slot
                real = tag >= 0
                held = jnp.maximum(tag, 0)
                passage = jnp.right_shift(held, per_bits)
                length = lens[passage]
                item_pass[item] = passage
                item_len[item] = length
                item_lane[item] = part * per_device + jnp.bitwise_and(held, per_device - 1)
                for tile in range(tiles):
                    work[count + tile] = item * tiles + tile
                count = count + jnp.where(real, jnp.right_shift(length + tile_tokens - 1, tile_tokens.bit_length() - 1), 0)
        for index in range(BLOCKS):
            work[count + index] = spare
        count = (count + BLOCKS - 1) // BLOCKS * BLOCKS
        for index in range(quad_sources * capacity * tiles // BLOCKS):
            work_quad[start // BLOCKS + index] = quad
        return count

    total = lax.fori_loop(0, quads, fill, 0)
    chunks = total // BLOCKS

    for part in range(parts):
        table_copy(part).wait()
        step_rows = 256

        def widen(index, carry, part=part):
            rows = pl.ds(pl.multiple_of(part * part_rows + index * step_rows, step_rows), step_rows)
            table[rows, :] = staged[rows, :].astype(jnp.float32)
            return carry

        lax.fori_loop(0, part_rows // step_rows, widen, 0)
    codes_copy.wait()
    for part in range(word_parts):
        words_copy(part).wait()

    sub = lax.broadcasted_iota(jnp.int32, (SUB, LANES), 0)
    position = jnp.concatenate([sub * FIELDS + field for field in range(FIELDS)], axis=0)
    lane_group = lax.broadcasted_iota(jnp.int32, (1, LANES), 1) // query_len
    level = [levels_ref[index : index + 1, :] for index in range(FIELDS)]

    def score(chunk):
        scores = jnp.dot(embed[...], query_t[work_quad[chunk]], preferred_element_type=jnp.float32)
        for index in range(BLOCKS):
            entry = work[chunk * BLOCKS + index]
            item, tile = jnp.right_shift(entry, tile_bits), jnp.bitwise_and(entry, tiles - 1)
            block = scores[index * tile_tokens : (index + 1) * tile_tokens]
            kept = jnp.where(position < item_len[item] - tile * tile_tokens, block, MASKED)
            best = jnp.max(kept, axis=0, keepdims=True)
            maxima[tile, pl.ds(item, 1), :] = jnp.where(lane_group == item_lane[item], best, 0.0)

    def decode(chunk):
        for index in range(BLOCKS):
            entry = work[chunk * BLOCKS + index]
            item, tile = jnp.right_shift(entry, tile_bits), jnp.bitwise_and(entry, tiles - 1)
            passage = item_pass[item]
            word = words[passage, pl.ds(pl.multiple_of(tile * SUB, SUB), SUB), :]
            dense = []
            for field in range(FIELDS):
                rows = jnp.zeros((SUB, LANES), jnp.float32)
                for row in range(SUB):
                    code = codes[passage, tile * tile_tokens + row * FIELDS + field]
                    rows = jnp.where(sub == row, table[pl.ds(code, SUB, stride=0), :], rows)
                low = jnp.bitwise_and(word, 1 << (2 * field)) != 0
                high = jnp.bitwise_and(word, 2 << (2 * field)) != 0
                residual = jnp.where(
                    high, jnp.where(low, level[3], level[2]), jnp.where(low, level[1], level[0])
                )
                dense.append(rows + residual)
            dense = jnp.concatenate(dense, axis=0)
            inverse = lax.rsqrt(jnp.sum(dense * dense, axis=1, keepdims=True) + 1e-06)
            embed[index * tile_tokens : (index + 1) * tile_tokens, :] = (dense * inverse).astype(jnp.bfloat16)

    @pl.when(chunks > 0)
    def _():
        decode(0)

        def both(chunk, carry):
            score(chunk - 1)
            decode(chunk)
            return carry

        lax.fori_loop(1, chunks, both, 0)
        score(chunks - 1)

    best = maxima[0, :items, :]
    for tile in range(1, tiles):
        best = jnp.maximum(best, maxima[tile, :items, :])
    sums = jnp.sum(best, axis=1, keepdims=True) / query_len
    width = out_ref.shape[1]
    item_down = lax.broadcasted_iota(jnp.int32, (items, width), 0)
    item_slot = lax.broadcasted_iota(jnp.int32, (items, width), 1)
    spread = jnp.where(item_down % capacity == item_slot, sums, 0.0)
    source_down = lax.broadcasted_iota(jnp.int32, (sources, items), 0)
    item_across = lax.broadcasted_iota(jnp.int32, (sources, items), 1)
    gather = (item_across // capacity == source_down).astype(jnp.float32)
    out_ref[...] = jnp.dot(
        gather, spread, precision=lax.Precision.HIGHEST, preferred_element_type=jnp.float32
    )


def owner_scores(me, cand_all, query_all, centroids, token_codes, resid_words, lengths, levels, sizes):
    capacity = sizes[4]
    sources, pairs = cand_all.shape
    cent_dev, width = centroids.shape
    pass_dev, plen = token_codes.shape
    packed = resid_words.shape[1]
    tiles = packed // SUB
    items = sources * capacity
    quads = query_all.shape[0] // LANES
    work_size = items * tiles + (quads + 1) * BLOCKS
    any_space = pl.BlockSpec(memory_space=pl.ANY)
    vmem = pl.BlockSpec(memory_space=pltpu.VMEM)
    tokens = items * plen
    return pl.pallas_call(
        functools.partial(score_kernel, sizes),
        in_specs=[pl.BlockSpec(memory_space=pltpu.SMEM), vmem, vmem, vmem] + [any_space] * 4,
        out_specs=vmem,
        out_shape=jax.ShapeDtypeStruct((sources, capacity), jnp.float32),
        scratch_shapes=[
            pltpu.VMEM((cent_dev, width), jnp.bfloat16),
            pltpu.VMEM((cent_dev + SUB, width), jnp.float32),
            pltpu.VMEM((pass_dev, packed, width), jnp.int32),
            pltpu.VMEM((quads, width, LANES), jnp.bfloat16),
            pltpu.VMEM((BLOCKS * SUB * FIELDS, width), jnp.bfloat16),
            pltpu.VMEM((tiles, items + SUB, LANES), jnp.float32),
            pltpu.VMEM((sources, LANES), jnp.int32),
            pltpu.SMEM((sources, LANES), jnp.int32),
            pltpu.SMEM((pass_dev, plen), jnp.int32),
            pltpu.SMEM((pass_dev,), jnp.int32),
            pltpu.SMEM((work_size,), jnp.int32),
            pltpu.SMEM((work_size // BLOCKS + items * tiles // quads,), jnp.int32),
            pltpu.SMEM((items + 1,), jnp.int32),
            pltpu.SMEM((items + 1,), jnp.int32),
            pltpu.SMEM((items + 1,), jnp.int32),
            pltpu.SemaphoreType.DMA((8,)),
            pltpu.SemaphoreType.DMA((4,)),
            pltpu.SemaphoreType.DMA((3,)),
        ],
        compiler_params=pltpu.CompilerParams(vmem_limit_bytes=48 * MIB),
        cost_estimate=pl.CostEstimate(
            flops=2 * tokens * width * LANES, bytes_accessed=2 * cent_dev * width * 2, transcendentals=tokens
        ),
        name="owner_scores",
    )(me, cand_all, levels, query_all, centroids, resid_words, token_codes, lengths)


def finish_kernel(best_ref, back_ref, target_ref, best_out, score_out):
    best = best_ref[0]
    for index in range(1, best_ref.shape[0]):
        best = jnp.maximum(best, best_ref[index])
    best_out[...] = best
    owners, capacity = back_ref.shape
    target = target_ref[...]
    owner = lax.broadcasted_iota(jnp.int32, (owners, target.shape[1]), 0)
    found = jnp.zeros(owner.shape, jnp.float32)
    for slot in range(capacity):
        found = found + jnp.where(owner * capacity + slot == target, back_ref[:, slot : slot + 1], 0.0)
    scores = jnp.sum(found, axis=0, keepdims=True)
    width = score_out.shape[1]
    for index in range(score_out.shape[0]):
        score_out[index : index + 1, :] = scores[:, index * width : (index + 1) * width]


def finish(best_all, back, target, per_device, cand_count):
    vmem = pl.BlockSpec(memory_space=pltpu.VMEM)
    return pl.pallas_call(
        finish_kernel,
        in_specs=[vmem] * 3,
        out_specs=[vmem] * 2,
        out_shape=[
            jax.ShapeDtypeStruct(best_all.shape[1:], jnp.float32),
            jax.ShapeDtypeStruct((per_device, cand_count), jnp.float32),
        ],
        name="finish",
    )(best_all, back, target)


def shards(queries, centroids, candidates, token_codes, resid_words, lengths, levels):
    group_rows, query_len, width = queries.shape
    pass_dev = token_codes.shape[0]
    per_device, cand_count = candidates.shape[2:]
    pair_count = per_device * cand_count
    cent_count = lax.axis_size("cent")
    group_count = lax.axis_size("grp")
    devices = cent_count * group_count
    capacity = max(2, 2 * pair_count // devices)
    sizes = (group_count, cent_count, per_device, query_len, capacity, pass_dev, cand_count)
    cand_row = candidates.reshape(1, pair_count)
    cand_all = lax.all_gather(cand_row, ("cent", "grp"), axis=0, tiled=True)
    query_all = lax.all_gather(queries, "grp", axis=0, tiled=True)
    me = (lax.axis_index("cent") * group_count + lax.axis_index("grp")).astype(jnp.int32).reshape(1)
    best, target = centroid_best(queries, cand_row, centroids, pass_dev, capacity)
    best_all = lax.all_gather(best, "cent", axis=0, tiled=False)
    query_rows = query_all.reshape(group_count * group_rows * query_len, width)
    totals = owner_scores(
        me, cand_all, query_rows, centroids, token_codes, resid_words, lengths, levels, sizes
    )
    back = lax.all_to_all(totals, ("cent", "grp"), split_axis=0, concat_axis=0, tiled=True)
    token_best, scores = finish(best_all, back, target, per_device, cand_count)
    return (token_best, scores.reshape(1, 1, per_device, cand_count))


def solution(mesh):
    placed = (
        P("grp", None, None),
        P("cent", None),
        P("grp", "cent", None, None),
        P(("cent", "grp"), None),
        P(("cent", "grp"), None, None),
        P(("cent", "grp")),
        P(),
    )
    return jax.shard_map(
        shards,
        mesh=mesh,
        in_specs=placed,
        out_specs=(P("grp", None), P("grp", "cent", None, None)),
        check_vma=False,
    )
```

time: 317 us -> 176 us (0.56); the launches traced: 312 us -> 174 us
  local copies, waits for them, and re-layouts: 182 us -> 7.69 us
  Pallas kernels: 0 us -> 69.8 us
  blocking collectives: 22.5 us -> 82.9 us
  other arithmetic: 42.9 us -> 0 us
  matrix products: 39.6 us -> 0 us
  waiting for transfers between devices: 7.24 us -> 0.01 us
    gather x10 -> x0, local copies, waits for them, and re-layouts: 126 us -> none  [the longest x1 114 us: shards(): jnp.take(centroids, flat_codes, axis=0)]
    all_gather x0 -> x3, blocking collectives: none -> 82.9 us  [the longest x1 41.2 us: shards(): cand_all = lax.all_gather(cand_row, ('cent', 'grp'), axis=0, tiled=True)]
    pallas_call x0 -> x3, Pallas kernels: none -> 69.8 us  [the longest x1 50.1 us: owner_scores(): pl.pallas_call(functools.partial(score_kernel, sizes), in_specs=[pl.Block...]
    eq x4 -> x0, local copies, waits for them, and re-layouts: 41.6 us -> none  [the longest x2 22.6 us: unpack_levels(): high_bit = jnp.bitwise_and(level_codes, 2) == 2]
    dot_general x17 -> x0, matrix products: 39.6 us -> none  [the longest x16 28.5 us: block_step(): lax.dot_general(flat_queries, centroid_block, (((1,), (1,)), ((), ())), p...]
    pmax x1 -> x0, blocking collectives: 22.5 us -> none  [shards(): token_best = lax.pmax(local_best, 'cent').reshape(group_rows, query_len)]
    convert_element_type x1 -> x0, other arithmetic: 14.1 us -> none  [dequantize(): return (dequantized * inverse_norm).astype(jnp.bfloat16)]
    reduce_sum x4 -> x0, other arithmetic: 13.7 us -> none  [the longest x1 13.3 us: dequantize(): jnp.sum(dequantized * dequantized, axis=-1, keepdims=True) + 1e-06]
  transfers between devices with their start and end apart: 3 -> 1, of which waited for: 1 -> 0; matrix products, arithmetic and copies ran while one was open for 79% -> 0% of each run, Pallas kernels for 0% -> 10%
where the time goes in v1:
time: 176 us; the launch traced here: 174 us
  blocking collectives  82.9 us (47%)
  Pallas kernels  69.8 us (40%)
  starting transfers between devices  13.2 us (8%)
  local copies, waits for them, and re-layouts  7.69 us (4%)
    pallas_call x1, Pallas kernels, owner_scores(): pl.pallas_call(functools.partial(score_kernel, sizes), in_specs=[pl.Block...  50.1 us
    all_gather x1, blocking collectives, shards(): cand_all = lax.all_gather(cand_row, ('cent', 'grp'), axis=0, tiled=True)  41.2 us
    all_gather x1, blocking collectives, shards(): best_all = lax.all_gather(best, 'cent', axis=0, tiled=False)  32.9 us
    pallas_call x1, Pallas kernels, centroid_best(): pl.pallas_call(functools.partial(best_kernel, pass_dev.bit_length() - 1,...  18.1 us
    all_to_all x1, starting transfers between devices, shards(): lax.all_to_all(totals, ('cent', 'grp'), split_axis=0, concat_axis=0, tile...  13.2 us
    all_gather x1, blocking collectives, shards(): query_all = lax.all_gather(queries, 'grp', axis=0, tiled=True)  8.83 us
    unnamed x17, local copies, waits for them, and re-layouts  7.6 us
  transfers between devices with their start and end apart: 1, of which 0 were waited for; matrix products, arithmetic and copies ran while one was open for 0% of the time, Pallas kernels for 10%

profile of v1, /device:TPU:0, one launch (start us, length us, event | category | flops | bytes accessed | tf_op | source)
XLA Modules:
  0.0 174.2 jit_solution(3766300947573316732)
XLA Ops:
  0.6 8.8 %all_gather.15 = bf16[64,32,128]{2,1,0:T(8,128)(2,1)S(1)} all-gather(bf16[16,32,128]{2,1,0:T(8,128)(2,1)} %param.7), channel_id=1, replica_groups=mesh['cent'=8,'grp'=4] {'grp'}, dimensions={0}, use_global_device_ids=true | all-gather | bytes 655360 | tf_op jit(solution)/shard_map/all_gather | solution.py:385
  9.5 0.8 reshape.27
  10.2 41.2 %all-gather.1 = s32[32,1,128]{2,1,0:T(1,128)S(1)} all-gather(s32[1,1,128]{2,1,0:T(1,128)S(1)} %reshape.27), channel_id=1, replica_groups=mesh['cent'=8,'grp'=4] {'cent','grp'}, dimensions={0}, use_global_device_ids=true | all-gather | bytes 16896 | tf_op jit(solution)/shard_map/all_gather | solution.py:384
  51.4 0.0 copy-start.1
  51.4 0.9 copy-done.1
  52.3 0.0 copy-start.3
  52.3 0.7 copy-done.3
  53.0 0.0 copy-start.4
  53.0 0.7 copy-done.4
  53.7 0.0 copy-start.7
  53.7 0.0 copy-start.2
  53.7 50.1 %owner_scores.1 = f32[32,8]{1,0:T(8,128)} custom-call(s32[1]{0:T(128)} %bitcast.2.me_ref, s32[32,128]{1,0:T(8,128)S(1)} %bitcast.12, f32[4,128]{1,0:T(4,128)S(1)} %copy-done.3, bf16[2048,128]{1,0:T(8,128)(2,1)S(1)} %bitcast.10, bf16[32768,128]{1,0:T(8,128)(2,1)} %cent_hbm.1, s32[512,32,128]{2,1,0:T(8,128)} %words_hbm.1, s32[512,128]{1,0:T(8,128)S(1)} %copy-done.1, ...), custom_call_target="tpu_custom_call" | custom-call | flops 1073741824 | bytes 16777216 | tf_op jit(solution)/shard_map/owner_scores/pallas_call | solution.py:309
  103.8 13.2 %all-to-all-start = ((f32[32,1,8]{2,1,0:T(1,128)}), f32[32,1,8]{2,1,0:T(1,128)S(1)}, u32[]{:S(2)}, u32[]{:S(2)}) async-start(f32[32,1,8]{2,1,0:T(1,128)} %bitcast.6), calls=%async_computation | async-start | bytes 32768 | tf_op jit(solution)/shard_map/all_to_all | solution.py:393
  117.0 0.0 copy-done.7
  117.0 0.1 reshape.22.cand_ref
  117.0 0.0 copy-done.2
  117.0 0.0 copy-start
  117.1 3.4 %copy-done = bf16[32768,128]{1,0:T(8,128)(2,1)S(1)} copy-done((bf16[32768,128]{1,0:T(8,128)(2,1)S(1)}, bf16[32768,128]{1,0:T(8,128)(2,1)}, u32[]{:S(2)}) %copy-start) | copy-done | bytes 8388632
  120.4 18.1 %centroid_best.1 = (f32[16,32]{1,0:T(8,128)S(1)}, s32[1,128]{1,0:T(1,128)S(1)}) custom-call(bf16[512,128]{1,0:T(8,128)(2,1)S(1)} %bitcast.11, s32[1,128]{1,0:T(1,128)S(1)} %reshape.22.cand_ref, bf16[32768,128]{1,0:T(8,128)(2,1)S(1)} %copy-done), custom_call_target="tpu_custom_call" | custom-call | flops 4294967296 | bytes 8388608 | tf_op jit(solution)/shard_map/centroid_best/pallas_call | solution.py:63
  138.6 0.0 copy-start.5
  138.6 0.5 copy-done.5
  139.1 32.9 %all-gather = f32[128,32]{1,0:T(8,128)} all-gather(f32[16,32]{1,0:T(8,128)S(1)} %get-tuple-element.6), channel_id=2, replica_groups=mesh['cent'=8,'grp'=4] {'cent'}, dimensions={0}, use_global_device_ids=true | all-gather | bytes 18432 | tf_op jit(solution)/shard_map/all_gather | solution.py:388
  172.0 0.0 all-to-all-done
  172.0 0.0 copy-start.6
  172.0 0.6 copy-done.6
  172.6 1.6 finish.1
Async XLA Ops:
  51.4 0.9 copy-start.1
  52.3 0.7 copy-start.3
  53.0 0.7 copy-start.4
  53.7 63.2 %copy-start.7 = (s32[1,1,2,64]{3,2,1,0:T(2,128)S(1)}, s32[1,1,2,64]{3,2,1,0:T(2,128)}, u32[]{:S(2)}) copy-start(s32[1,1,2,64]{3,2,1,0:T(2,128)} %param.9) | copy-start | bytes 1540
  53.7 63.3 %copy-start.2 = (bf16[16,32,128]{2,1,0:T(8,128)(2,1)S(1)}, bf16[16,32,128]{2,1,0:T(8,128)(2,1)}, u32[]{:S(2)}) copy-start(bf16[16,32,128]{2,1,0:T(8,128)(2,1)} %param.7) | copy-start | bytes 393220
  103.8 68.2 %all-to-all-start = ((f32[32,1,8]{2,1,0:T(1,128)}), f32[32,1,8]{2,1,0:T(1,128)S(1)}, u32[]{:S(2)}, u32[]{:S(2)}) async-start(f32[32,1,8]{2,1,0:T(1,128)} %bitcast.6), calls=%async_computation | async-start | bytes 32768 | tf_op jit(solution)/shard_map/all_to_all | solution.py:393
  117.0 3.4 %copy-start = (bf16[32768,128]{1,0:T(8,128)(2,1)S(1)}, bf16[32768,128]{1,0:T(8,128)(2,1)}, u32[]{:S(2)}) copy-start(bf16[32768,128]{1,0:T(8,128)(2,1)} %cent_hbm.1) | copy-start | bytes 25165828
  138.6 0.5 copy-start.5
  172.0 0.6 copy-start.6

commit v2 on v1

--- a/solution.py
+++ b/solution.py
@@ -11,7 +11,8 @@
 LANES = 128
 SUB = 8
 FIELDS = 4
-BLOCKS = 8
+BLOCKS = 16
+ALIGN = 8
 MIB = 1 << 20
 
 
@@ -22,15 +23,39 @@
     return jnp.sum(jnp.where(down == across, row, 0.0), axis=1, keepdims=True)
 
 
+def one_row(rows):
+    return jnp.concatenate([rows[index : index + 1, :] for index in range(rows.shape[0])], axis=1)
+
+
+def send_kernel(q_ref, cand_ref, ids_ref, sent_ref):
+    ids_ref[...] = jnp.broadcast_to(one_row(cand_ref[...]), ids_ref.shape)
+    for index in range(sent_ref.shape[0]):
+        sent_ref[index] = q_ref[...]
+
+
+def send_blocks(query_rows, cand, devices, group_count):
+    vmem = pl.BlockSpec(memory_space=pltpu.VMEM)
+    return pl.pallas_call(
+        send_kernel,
+        in_specs=[vmem] * 2,
+        out_specs=[vmem] * 2,
+        out_shape=[
+            jax.ShapeDtypeStruct((devices, cand.size), jnp.int32),
+            jax.ShapeDtypeStruct((group_count,) + query_rows.shape, query_rows.dtype),
+        ],
+        name="send_blocks",
+    )(query_rows, cand)
+
+
 def best_kernel(owner_shift, capacity, q_ref, cand_ref, cent_ref, best_ref, target_ref, qt_ref, acc_ref):
     step = pl.program_id(0)
-    rows = 512
+    rows = min(cent_ref.shape[0], 2048)
 
     @pl.when(step == 0)
     def _():
         qt_ref[...] = jnp.transpose(q_ref[...].astype(jnp.float32)).astype(jnp.bfloat16)
         acc_ref[...] = jnp.full(acc_ref.shape, -jnp.inf, jnp.float32)
-        owners = jnp.right_shift(cand_ref[...], owner_shift).astype(jnp.float32)
+        owners = jnp.right_shift(one_row(cand_ref[...]), owner_shift).astype(jnp.float32)
         pairs = owners.shape[1]
         earlier = lax.broadcasted_iota(jnp.int32, (pairs, pairs), 0) < lax.broadcasted_iota(
             jnp.int32, (pairs, pairs), 1
@@ -49,49 +74,48 @@
     @pl.when(step == pl.num_programs(0) - 1)
     def _():
         best = jnp.max(acc_ref[...], axis=0, keepdims=True)
-        width = best_ref.shape[1]
         for index in range(best_ref.shape[0]):
-            best_ref[index : index + 1, :] = best[:, index * width : (index + 1) * width]
-
-
-def centroid_best(queries, cand_row, centroids, pass_dev, capacity):
-    group_rows, query_len, width = queries.shape
-    tokens = group_rows * query_len
+            best_ref[index : index + 1, :] = best[:, index * LANES : (index + 1) * LANES]
+
+
+def centroid_best(query_rows, cand, centroids, pass_dev, capacity):
+    tokens, width = query_rows.shape
     cent_dev = centroids.shape[0]
     block = min(cent_dev, 4096)
-    pairs = cand_row.shape[1]
+    pairs = cand.size
     return pl.pallas_call(
         functools.partial(best_kernel, pass_dev.bit_length() - 1, capacity),
         grid=(cent_dev // block,),
         in_specs=[
             pl.BlockSpec((tokens, width), lambda i: (0, 0)),
+            pl.BlockSpec(cand.shape, lambda i: (0, 0)),
+            pl.BlockSpec((block, width), lambda i: (i, 0)),
+        ],
+        out_specs=[
+            pl.BlockSpec((tokens // LANES, LANES), lambda i: (0, 0)),
             pl.BlockSpec((1, pairs), lambda i: (0, 0)),
-            pl.BlockSpec((block, width), lambda i: (i, 0)),
-        ],
-        out_specs=[
-            pl.BlockSpec((group_rows, query_len), lambda i: (0, 0)),
-            pl.BlockSpec((1, pairs), lambda i: (0, 0)),
         ],
         out_shape=[
-            jax.ShapeDtypeStruct((group_rows, query_len), jnp.float32),
+            jax.ShapeDtypeStruct((tokens // LANES, LANES), jnp.float32),
             jax.ShapeDtypeStruct((1, pairs), jnp.int32),
         ],
         scratch_shapes=[
             pltpu.VMEM((width, tokens), jnp.bfloat16),
             pltpu.VMEM((SUB, tokens), jnp.float32),
         ],
-        compiler_params=pltpu.CompilerParams(vmem_limit_bytes=24 * MIB),
+        compiler_params=pltpu.CompilerParams(vmem_limit_bytes=56 * MIB),
         cost_estimate=pl.CostEstimate(
             flops=2 * tokens * cent_dev * width, bytes_accessed=2 * cent_dev * width, transcendentals=0
         ),
         name="centroid_best",
-    )(queries.reshape(tokens, width), cand_row, centroids)
+    )(query_rows, cand, centroids)
 
 
 def score_kernel(
     sizes,
     me_ref,
     cand_ref,
+    best_ref,
     levels_ref,
     query_ref,
     cent_hbm,
@@ -127,24 +151,26 @@
     quads = sources // quad_sources
     per_bits = per_device.bit_length() - 1
     tile_bits = tiles.bit_length() - 1
-    parts = table_sem.shape[0]
-    part_rows = staged.shape[0] // parts
+    part_rows = staged.shape[0] // quads
     word_parts = words_sem.shape[0]
     part_pass = pass_dev // word_parts
 
     def table_copy(part):
-        rows = pl.ds(part * part_rows, part_rows)
+        rows = pl.ds(pl.multiple_of(part * part_rows, part_rows), part_rows)
         return pltpu.make_async_copy(cent_hbm.at[rows, :], staged.at[rows, :], table_sem.at[part])
 
     def words_copy(part):
         rows = pl.ds(part * part_pass, part_pass)
         return pltpu.make_async_copy(words_hbm.at[rows], words.at[rows], words_sem.at[part])
 
+    def start_table(part, carry):
+        table_copy(part).start()
+        return carry
+
     lens_copy = pltpu.make_async_copy(lens_hbm, lens, small_sem.at[0])
     codes_copy = pltpu.make_async_copy(codes_hbm, codes, small_sem.at[1])
     lens_copy.start()
-    for part in range(parts):
-        table_copy(part).start()
+    lax.fori_loop(0, quads, start_table, 0)
     codes_copy.start()
     for part in range(word_parts):
         words_copy(part).start()
@@ -169,12 +195,6 @@
     ids_copy = pltpu.make_async_copy(ids_vmem, ids, small_sem.at[2])
     ids_copy.start()
 
-    def turn(quad, carry):
-        block = query_ref[pl.ds(pl.multiple_of(quad * LANES, LANES), LANES), :]
-        query_t[quad] = jnp.transpose(block.astype(jnp.float32)).astype(jnp.bfloat16)
-        return carry
-
-    lax.fori_loop(0, quads, turn, 0)
     maxima[...] = jnp.full(maxima.shape, MASKED, jnp.float32)
     embed[...] = jnp.zeros(embed.shape, embed.dtype)
     lens_copy.wait()
@@ -185,7 +205,12 @@
     item_lane[items] = -1
     spare = items * tiles
 
-    def fill(quad, count):
+    def prepare(quad, count):
+        table_copy(quad).wait()
+        rows = pl.ds(pl.multiple_of(quad * part_rows, part_rows), part_rows)
+        table[rows, :] = staged[rows, :].astype(jnp.float32)
+        block = query_ref[pl.ds(pl.multiple_of(quad * LANES, LANES), LANES), :]
+        query_t[quad] = jnp.transpose(block.astype(jnp.float32)).astype(jnp.bfloat16)
         start = count
         group = quad // (cent_count // quad_sources)
         cent = (quad % (cent_count // quad_sources)) * quad_sources
@@ -204,26 +229,19 @@
                 for tile in range(tiles):
                     work[count + tile] = item * tiles + tile
                 count = count + jnp.where(real, jnp.right_shift(length + tile_tokens - 1, tile_tokens.bit_length() - 1), 0)
-        for index in range(BLOCKS):
+        for index in range(ALIGN):
             work[count + index] = spare
-        count = (count + BLOCKS - 1) // BLOCKS * BLOCKS
-        for index in range(quad_sources * capacity * tiles // BLOCKS):
-            work_quad[start // BLOCKS + index] = quad
+        count = (count + ALIGN - 1) // ALIGN * ALIGN
+        for index in range(quad_sources * capacity * tiles // ALIGN):
+            work_quad[start // ALIGN + index] = quad
         return count
 
-    total = lax.fori_loop(0, quads, fill, 0)
-    chunks = total // BLOCKS
-
-    for part in range(parts):
-        table_copy(part).wait()
-        step_rows = 256
-
-        def widen(index, carry, part=part):
-            rows = pl.ds(pl.multiple_of(part * part_rows + index * step_rows, step_rows), step_rows)
-            table[rows, :] = staged[rows, :].astype(jnp.float32)
-            return carry
-
-        lax.fori_loop(0, part_rows // step_rows, widen, 0)
+    total = lax.fori_loop(0, quads, prepare, 0)
+    for index in range(BLOCKS):
+        work[total + index] = spare
+    for index in range(BLOCKS // ALIGN):
+        work_quad[total // ALIGN + index] = 0
+    chunks = (total + BLOCKS - 1) // BLOCKS
     codes_copy.wait()
     for part in range(word_parts):
         words_copy(part).wait()
@@ -234,11 +252,16 @@
     level = [levels_ref[index : index + 1, :] for index in range(FIELDS)]
 
     def score(chunk):
-        scores = jnp.dot(embed[...], query_t[work_quad[chunk]], preferred_element_type=jnp.float32)
+        scores = []
+        for part in range(BLOCKS // ALIGN):
+            rows = embed[part * ALIGN * tile_tokens : (part + 1) * ALIGN * tile_tokens, :]
+            quad = work_quad[chunk * (BLOCKS // ALIGN) + part]
+            scores.append(jnp.dot(rows, query_t[quad], preferred_element_type=jnp.float32))
         for index in range(BLOCKS):
             entry = work[chunk * BLOCKS + index]
             item, tile = jnp.right_shift(entry, tile_bits), jnp.bitwise_and(entry, tiles - 1)
-            block = scores[index * tile_tokens : (index + 1) * tile_tokens]
+            inner = index % ALIGN
+            block = scores[index // ALIGN][inner * tile_tokens : (inner + 1) * tile_tokens]
             kept = jnp.where(position < item_len[item] - tile * tile_tokens, block, MASKED)
             best = jnp.max(kept, axis=0, keepdims=True)
             maxima[tile, pl.ds(item, 1), :] = jnp.where(lane_group == item_lane[item], best, 0.0)
@@ -250,10 +273,11 @@
             passage = item_pass[item]
             word = words[passage, pl.ds(pl.multiple_of(tile * SUB, SUB), SUB), :]
             dense = []
+            start = passage * (tiles * tile_tokens) + tile * tile_tokens
             for field in range(FIELDS):
                 rows = jnp.zeros((SUB, LANES), jnp.float32)
                 for row in range(SUB):
-                    code = codes[passage, tile * tile_tokens + row * FIELDS + field]
+                    code = codes[start + (row * FIELDS + field)]
                     rows = jnp.where(sub == row, table[pl.ds(code, SUB, stride=0), :], rows)
                 low = jnp.bitwise_and(word, 1 << (2 * field)) != 0
                 high = jnp.bitwise_and(word, 2 << (2 * field)) != 0
@@ -281,19 +305,22 @@
     for tile in range(1, tiles):
         best = jnp.maximum(best, maxima[tile, :items, :])
     sums = jnp.sum(best, axis=1, keepdims=True) / query_len
-    width = out_ref.shape[1]
-    item_down = lax.broadcasted_iota(jnp.int32, (items, width), 0)
-    item_slot = lax.broadcasted_iota(jnp.int32, (items, width), 1)
+    item_down = lax.broadcasted_iota(jnp.int32, (items, LANES), 0)
+    item_slot = lax.broadcasted_iota(jnp.int32, (items, LANES), 1)
     spread = jnp.where(item_down % capacity == item_slot, sums, 0.0)
     source_down = lax.broadcasted_iota(jnp.int32, (sources, items), 0)
     item_across = lax.broadcasted_iota(jnp.int32, (sources, items), 1)
     gather = (item_across // capacity == source_down).astype(jnp.float32)
-    out_ref[...] = jnp.dot(
+    by_source = jnp.dot(
         gather, spread, precision=lax.Precision.HIGHEST, preferred_element_type=jnp.float32
     )
-
-
-def owner_scores(me, cand_all, query_all, centroids, token_codes, resid_words, lengths, levels, sizes):
+    rows_best = best_ref.shape[0]
+    for source in range(sources):
+        out_ref[source, :rows_best, :] = best_ref[...]
+        out_ref[source, rows_best : rows_best + 1, :] = by_source[source : source + 1, :]
+
+
+def owner_scores(me, cand_all, best, query_all, centroids, token_codes, resid_words, lengths, levels, sizes):
     capacity = sizes[4]
     sources, pairs = cand_all.shape
     cent_dev, width = centroids.shape
@@ -302,15 +329,16 @@
     tiles = packed // SUB
     items = sources * capacity
     quads = query_all.shape[0] // LANES
-    work_size = items * tiles + (quads + 1) * BLOCKS
+    work_size = items * tiles + quads * ALIGN + BLOCKS
+    reply_rows = (best.shape[0] + SUB) // SUB * SUB
     any_space = pl.BlockSpec(memory_space=pl.ANY)
     vmem = pl.BlockSpec(memory_space=pltpu.VMEM)
     tokens = items * plen
     return pl.pallas_call(
         functools.partial(score_kernel, sizes),
-        in_specs=[pl.BlockSpec(memory_space=pltpu.SMEM), vmem, vmem, vmem] + [any_space] * 4,
+        in_specs=[pl.BlockSpec(memory_space=pltpu.SMEM), vmem, vmem, vmem, vmem] + [any_space] * 4,
         out_specs=vmem,
-        out_shape=jax.ShapeDtypeStruct((sources, capacity), jnp.float32),
+        out_shape=jax.ShapeDtypeStruct((sources, reply_rows, LANES), jnp.float32),
         scratch_shapes=[
             pltpu.VMEM((cent_dev, width), jnp.bfloat16),
             pltpu.VMEM((cent_dev + SUB, width), jnp.float32),
@@ -320,54 +348,62 @@
             pltpu.VMEM((tiles, items + SUB, LANES), jnp.float32),
             pltpu.VMEM((sources, LANES), jnp.int32),
             pltpu.SMEM((sources, LANES), jnp.int32),
-            pltpu.SMEM((pass_dev, plen), jnp.int32),
+            pltpu.SMEM((pass_dev * plen,), jnp.int32),
             pltpu.SMEM((pass_dev,), jnp.int32),
             pltpu.SMEM((work_size,), jnp.int32),
-            pltpu.SMEM((work_size // BLOCKS + items * tiles // quads,), jnp.int32),
+            pltpu.SMEM((work_size // ALIGN + items * tiles // quads,), jnp.int32),
             pltpu.SMEM((items + 1,), jnp.int32),
             pltpu.SMEM((items + 1,), jnp.int32),
             pltpu.SMEM((items + 1,), jnp.int32),
-            pltpu.SemaphoreType.DMA((8,)),
+            pltpu.SemaphoreType.DMA((quads,)),
             pltpu.SemaphoreType.DMA((4,)),
             pltpu.SemaphoreType.DMA((3,)),
         ],
-        compiler_params=pltpu.CompilerParams(vmem_limit_bytes=48 * MIB),
+        compiler_params=pltpu.CompilerParams(vmem_limit_bytes=56 * MIB),
         cost_estimate=pl.CostEstimate(
             flops=2 * tokens * width * LANES, bytes_accessed=2 * cent_dev * width * 2, transcendentals=tokens
         ),
         name="owner_scores",
-    )(me, cand_all, levels, query_all, centroids, resid_words, token_codes, lengths)
-
-
-def finish_kernel(best_ref, back_ref, target_ref, best_out, score_out):
-    best = best_ref[0]
-    for index in range(1, best_ref.shape[0]):
-        best = jnp.maximum(best, best_ref[index])
-    best_out[...] = best
-    owners, capacity = back_ref.shape
+    )(me, cand_all, best, levels, query_all, centroids, resid_words, token_codes.reshape(pass_dev * plen), lengths)
+
+
+def finish_kernel(sizes, me_ref, back_ref, target_ref, best_out, score_out):
+    group_count, cent_count, _, query_len, capacity, _, _ = sizes
+    group = jnp.bitwise_and(me_ref[0], group_count - 1)
+    rows_best = best_out.shape[0] * query_len // LANES
+    best = back_ref[group, :rows_best, :]
+    for cent in range(1, cent_count):
+        best = jnp.maximum(best, back_ref[cent * group_count + group, :rows_best, :])
+    for index in range(best_out.shape[0]):
+        row, lane = divmod(index * query_len, LANES)
+        best_out[index : index + 1, :] = best[row : row + 1, lane : lane + query_len]
+    back = back_ref[...]
+    row = lax.broadcasted_iota(jnp.int32, back.shape, 1)
+    back = jnp.sum(jnp.where(row == rows_best, back, 0.0), axis=1)
     target = target_ref[...]
-    owner = lax.broadcasted_iota(jnp.int32, (owners, target.shape[1]), 0)
+    owner = lax.broadcasted_iota(jnp.int32, (back.shape[0], target.shape[1]), 0)
     found = jnp.zeros(owner.shape, jnp.float32)
     for slot in range(capacity):
-        found = found + jnp.where(owner * capacity + slot == target, back_ref[:, slot : slot + 1], 0.0)
+        found = found + jnp.where(owner * capacity + slot == target, back[:, slot : slot + 1], 0.0)
     scores = jnp.sum(found, axis=0, keepdims=True)
     width = score_out.shape[1]
     for index in range(score_out.shape[0]):
         score_out[index : index + 1, :] = scores[:, index * width : (index + 1) * width]
 
 
-def finish(best_all, back, target, per_device, cand_count):
+def finish(me, back, target, group_rows, sizes):
+    _, _, per_device, query_len, _, _, cand_count = sizes
     vmem = pl.BlockSpec(memory_space=pltpu.VMEM)
     return pl.pallas_call(
-        finish_kernel,
-        in_specs=[vmem] * 3,
+        functools.partial(finish_kernel, sizes),
+        in_specs=[pl.BlockSpec(memory_space=pltpu.SMEM), vmem, vmem],
         out_specs=[vmem] * 2,
         out_shape=[
-            jax.ShapeDtypeStruct(best_all.shape[1:], jnp.float32),
+            jax.ShapeDtypeStruct((group_rows, query_len), jnp.float32),
             jax.ShapeDtypeStruct((per_device, cand_count), jnp.float32),
         ],
         name="finish",
-    )(best_all, back, target)
+    )(me, back, target)
 
 
 def shards(queries, centroids, candidates, token_codes, resid_words, lengths, levels):
@@ -380,18 +416,19 @@
     devices = cent_count * group_count
     capacity = max(2, 2 * pair_count // devices)
     sizes = (group_count, cent_count, per_device, query_len, capacity, pass_dev, cand_count)
-    cand_row = candidates.reshape(1, pair_count)
-    cand_all = lax.all_gather(cand_row, ("cent", "grp"), axis=0, tiled=True)
-    query_all = lax.all_gather(queries, "grp", axis=0, tiled=True)
+    cand = candidates.reshape(per_device, cand_count)
+    query_rows = queries.reshape(group_rows * query_len, width)
     me = (lax.axis_index("cent") * group_count + lax.axis_index("grp")).astype(jnp.int32).reshape(1)
-    best, target = centroid_best(queries, cand_row, centroids, pass_dev, capacity)
-    best_all = lax.all_gather(best, "cent", axis=0, tiled=False)
-    query_rows = query_all.reshape(group_count * group_rows * query_len, width)
-    totals = owner_scores(
-        me, cand_all, query_rows, centroids, token_codes, resid_words, lengths, levels, sizes
-    )
-    back = lax.all_to_all(totals, ("cent", "grp"), split_axis=0, concat_axis=0, tiled=True)
-    token_best, scores = finish(best_all, back, target, per_device, cand_count)
+    ids_sent, rows_sent = send_blocks(query_rows, cand, devices, group_count)
+    cand_all = lax.all_to_all(ids_sent, ("cent", "grp"), split_axis=0, concat_axis=0, tiled=True)
+    query_all = lax.all_to_all(rows_sent, "grp", split_axis=0, concat_axis=0, tiled=True)
+    best, target = centroid_best(query_rows, cand, centroids, pass_dev, capacity)
+    query_all = query_all.reshape(group_count * group_rows * query_len, width)
+    reply = owner_scores(
+        me, cand_all, best, query_all, centroids, token_codes, resid_words, lengths, levels, sizes
+    )
+    back = lax.all_to_all(reply, ("cent", "grp"), split_axis=0, concat_axis=0, tiled=True)
+    token_best, scores = finish(me, back, target, group_rows, sizes)
     return (token_best, scores.reshape(1, 1, per_device, cand_count))
 
 

time: 176 us -> 84.5 us (0.48); the launches traced: 174 us -> 84.7 us
  blocking collectives: 82.9 us -> 16.1 us
  Pallas kernels: 69.8 us -> 49.2 us
  waiting for transfers between devices: 0.01 us -> 7.14 us
  local copies, waits for them, and re-layouts: 7.69 us -> 0.8 us
  starting transfers between devices: 13.2 us -> 10.8 us
    all_gather x3 -> x0, blocking collectives: 82.9 us -> none  [the longest x1 41.2 us: shards(): cand_all = lax.all_gather(cand_row, ('cent', 'grp'), axis=0, tiled=True)]
    pallas_call x1, Pallas kernels: 50.1 us -> 32.1 us  [owner_scores(): pl.pallas_call(functools.partial(score_kernel, sizes), in_specs=[pl.Block...]
    all_to_all x0 -> x1, blocking collectives: none -> 16.1 us  [shards(): lax.all_to_all(reply, ('cent', 'grp'), split_axis=0, concat_axis=0, tiled...]
    all_to_all x1 -> x2, waiting for transfers between devices: 0.01 us -> 7.14 us  [the longest x1 7.14 us: shards(): lax.all_to_all(ids_sent, ('cent', 'grp'), split_axis=0, concat_axis=0, ti...]
    unnamed x17 -> x4, local copies, waits for them, and re-layouts: 7.6 us -> 0.8 us
    pallas_call x1, Pallas kernels: 18.1 us -> 13.4 us  [centroid_best(): pl.pallas_call(functools.partial(best_kernel, pass_dev.bit_length() - 1,...]
    all_to_all x1 -> x2, starting transfers between devices: 13.2 us -> 10.8 us  [the longest x1 7.3 us: shards(): lax.all_to_all(ids_sent, ('cent', 'grp'), split_axis=0, concat_axis=0, ti...]
    pallas_call x1 -> x2, Pallas kernels: 1.61 us -> 3.7 us  [the longest x1 1.92 us: finish(): pl.pallas_call(functools.partial(finish_kernel, sizes), in_specs=[pl.Bloc...]
  transfers between devices with their start and end apart: 1 -> 2, of which waited for: 0 -> 1; matrix products, arithmetic and copies ran while one was open for 0% -> 0% of each run, Pallas kernels for 10% -> 16%
where the time goes in v2:
time: 84.5 us; the launch traced here: 84.7 us
  Pallas kernels  49.2 us (58%)
  blocking collectives  16.1 us (19%)
  starting transfers between devices  10.8 us (13%)
  waiting for transfers between devices  7.14 us (8%)
    pallas_call x1, Pallas kernels, owner_scores(): pl.pallas_call(functools.partial(score_kernel, sizes), in_specs=[pl.Block...  32.1 us
    all_to_all x1, blocking collectives, shards(): lax.all_to_all(reply, ('cent', 'grp'), split_axis=0, concat_axis=0, tiled...  16.1 us
    pallas_call x1, Pallas kernels, centroid_best(): pl.pallas_call(functools.partial(best_kernel, pass_dev.bit_length() - 1,...  13.4 us
    all_to_all x1, starting transfers between devices, shards(): lax.all_to_all(ids_sent, ('cent', 'grp'), split_axis=0, concat_axis=0, ti...  7.3 us
    all_to_all x1, waiting for transfers between devices, shards(): lax.all_to_all(ids_sent, ('cent', 'grp'), split_axis=0, concat_axis=0, ti...  7.14 us
    all_to_all x1, starting transfers between devices, shards(): lax.all_to_all(rows_sent, 'grp', split_axis=0, concat_axis=0, tiled=True)  3.47 us
    pallas_call x1, Pallas kernels, finish(): pl.pallas_call(functools.partial(finish_kernel, sizes), in_specs=[pl.Bloc...  1.92 us
    pallas_call x1, Pallas kernels, send_blocks(): pl.pallas_call(send_kernel, in_specs=[vmem] * 2, out_specs=[vmem] * 2, ou...  1.78 us
  transfers between devices with their start and end apart: 2, of which 1 were waited for; matrix products, arithmetic and copies ran while one was open for 0% of the time, Pallas kernels for 16%

profile of v2, /device:TPU:0, one launch (start us, length us, event | category | flops | bytes accessed | tf_op | source)
XLA Modules:
  0.0 84.7 jit_solution(10408408515910390360)
XLA Ops:
  0.6 1.8 %send_blocks.1 = (s32[32,128]{1,0:T(8,128)}, bf16[4,512,128]{2,1,0:T(8,128)(2,1)}) custom-call(bf16[512,128]{1,0:T(8,128)(2,1)} %bitcast.12, s32[2,64]{1,0:T(2,128)} %bitcast.16), custom_call_target="tpu_custom_call" | custom-call | tf_op jit(solution)/shard_map/send_blocks/pallas_call | solution.py:38
  2.4 7.3 %all-to-all-start = ((s32[32,1,128]{2,1,0:T(1,128)}), s32[32,1,128]{2,1,0:T(1,128)S(1)}, u32[]{:S(2)}, u32[]{:S(2)}) async-start(s32[32,1,128]{2,1,0:T(1,128)} %bitcast.15), calls=%async_computation | async-start | bytes 32768 | tf_op jit(solution)/shard_map/all_to_all | solution.py:423
  9.7 7.1 %all-to-all-done = s32[32,1,128]{2,1,0:T(1,128)S(1)} async-done(((s32[32,1,128]{2,1,0:T(1,128)}), s32[32,1,128]{2,1,0:T(1,128)S(1)}, u32[]{:S(2)}, u32[]{:S(2)}) %all-to-all-start) | async-done | bytes 16416 | tf_op jit(solution)/shard_map/all_to_all | solution.py:423
  16.9 0.0 copy-start.1
  16.9 3.5 %all-to-all-start.1 = ((bf16[4,512,128]{2,1,0:T(8,128)(2,1)}), bf16[4,512,128]{2,1,0:T(8,128)(2,1)S(1)}, u32[]{:S(2)}, u32[]{:S(2)}) async-start(bf16[4,512,128]{2,1,0:T(8,128)(2,1)} %get-tuple-element.10), calls=%async_computation.1 | async-start | bytes 1048576 | tf_op jit(solution)/shard_map/all_to_all | solution.py:424
  20.3 13.4 %centroid_best.1 = (f32[4,128]{1,0:T(4,128)}, s32[1,128]{1,0:T(1,128)}) custom-call(bf16[512,128]{1,0:T(8,128)(2,1)} %bitcast.13, s32[2,64]{1,0:T(2,128)} %bitcast.17, bf16[32768,128]{1,0:T(8,128)(2,1)} %cent_hbm.1), custom_call_target="tpu_custom_call" | custom-call | flops 4294967296 | bytes 8388608 | tf_op jit(solution)/shard_map/centroid_best/pallas_call | solution.py:86
  33.7 0.0 copy-done.1
  33.7 0.0 all-to-all-done.1
  33.7 0.0 copy-start
  33.8 0.8 copy-done
  34.5 32.1 %owner_scores.1 = f32[32,8,128]{2,1,0:T(8,128)} custom-call(s32[1]{0:T(128)} %bitcast.me_ref, s32[32,128]{1,0:T(8,128)} %bitcast.14, f32[4,128]{1,0:T(4,128)} %get-tuple-element.9.best_ref, f32[4,128]{1,0:T(4,128)} %levels_ref.1, bf16[2048,128]{1,0:T(8,128)(2,1)} %bitcast.10, bf16[32768,128]{1,0:T(8,128)(2,1)} %cent_hbm.1, s32[512,32,128]{2,1,0:T(8,128)} %words_hbm.1, ...), custom_call_target="tpu_custom_call" | custom-call | flops 1073741824 | bytes 16777216 | tf_op jit(solution)/shard_map/owner_scores/pallas_call | solution.py:337
  66.7 16.1 %all_to_all.21.back_ref = f32[32,8,128]{2,1,0:T(8,128)} all-to-all(f32[32,8,128]{2,1,0:T(8,128)} %owner_scores.1), channel_id=1, replica_groups=mesh['cent'=8,'grp'=4] {'cent','grp'}, dimensions={0} | all-to-all | bytes 262144 | tf_op jit(solution)/shard_map/all_to_all | solution.py:430
  82.8 1.9 %finish.1 = (f32[16,32]{1,0:T(8,128)}, f32[2,64]{1,0:T(2,128)}) custom-call(s32[1]{0:T(128)} %bitcast.me_ref, f32[32,8,128]{2,1,0:T(8,128)} %all_to_all.21.back_ref, s32[1,128]{1,0:T(1,128)} %get-tuple-element.11.target_ref), custom_call_target="tpu_custom_call" | custom-call | tf_op jit(solution)/shard_map/finish/pallas_call | solution.py:397
Async XLA Ops:
  2.4 14.4 %all-to-all-start = ((s32[32,1,128]{2,1,0:T(1,128)}), s32[32,1,128]{2,1,0:T(1,128)S(1)}, u32[]{:S(2)}, u32[]{:S(2)}) async-start(s32[32,1,128]{2,1,0:T(1,128)} %bitcast.15), calls=%async_computation | async-start | bytes 32768 | tf_op jit(solution)/shard_map/all_to_all | solution.py:423
  16.9 16.9 %copy-start.1 = (s32[32,1,128]{2,1,0:T(1,128)}, s32[32,1,128]{2,1,0:T(1,128)S(1)}, u32[]{:S(2)}) copy-start(s32[32,1,128]{2,1,0:T(1,128)S(1)} %all-to-all-done) | copy-start | bytes 49156
  16.9 16.9 %all-to-all-start.1 = ((bf16[4,512,128]{2,1,0:T(8,128)(2,1)}), bf16[4,512,128]{2,1,0:T(8,128)(2,1)S(1)}, u32[]{:S(2)}, u32[]{:S(2)}) async-start(bf16[4,512,128]{2,1,0:T(8,128)(2,1)} %get-tuple-element.10), calls=%async_computation.1 | async-start | bytes 1048576 | tf_op jit(solution)/shard_map/all_to_all | solution.py:424
  33.7 0.8 copy-start

commit v3 on v2

--- a/solution.py
+++ b/solution.py
@@ -13,6 +13,8 @@
 FIELDS = 4
 BLOCKS = 16
 ALIGN = 8
+DIGITS = 3
+DIGIT_ROWS = 16
 MIB = 1 << 20
 
 
@@ -27,29 +29,34 @@
     return jnp.concatenate([rows[index : index + 1, :] for index in range(rows.shape[0])], axis=1)
 
 
-def send_kernel(q_ref, cand_ref, ids_ref, sent_ref):
-    ids_ref[...] = jnp.broadcast_to(one_row(cand_ref[...]), ids_ref.shape)
+def send_kernel(group_bits, me_ref, q_ref, cand_ref, sent_ref):
+    own_rows = sent_ref.shape[1] - DIGIT_ROWS
+    start = jnp.right_shift(me_ref[0], group_bits) * own_rows
+    rows = q_ref[pl.ds(pl.multiple_of(start, own_rows), own_rows), :]
+    ids = one_row(cand_ref[...])
+    digits = [jnp.bitwise_and(jnp.right_shift(ids, 8 * index), 255) for index in range(DIGITS)]
+    digits.append(jnp.zeros((DIGIT_ROWS - DIGITS, ids.shape[1]), jnp.int32))
+    digits = jnp.concatenate(digits, axis=0).astype(jnp.float32).astype(jnp.bfloat16)
     for index in range(sent_ref.shape[0]):
-        sent_ref[index] = q_ref[...]
-
-
-def send_blocks(query_rows, cand, devices, group_count):
+        sent_ref[index, :own_rows, :] = rows
+        sent_ref[index, own_rows:, :] = digits
+
+
+def send_blocks(me, query_rows, cand, devices, own_rows, group_count):
+    width = query_rows.shape[1]
     vmem = pl.BlockSpec(memory_space=pltpu.VMEM)
     return pl.pallas_call(
-        send_kernel,
-        in_specs=[vmem] * 2,
-        out_specs=[vmem] * 2,
-        out_shape=[
-            jax.ShapeDtypeStruct((devices, cand.size), jnp.int32),
-            jax.ShapeDtypeStruct((group_count,) + query_rows.shape, query_rows.dtype),
-        ],
+        functools.partial(send_kernel, group_count.bit_length() - 1),
+        in_specs=[pl.BlockSpec(memory_space=pltpu.SMEM), vmem, vmem],
+        out_specs=vmem,
+        out_shape=jax.ShapeDtypeStruct((devices, own_rows + DIGIT_ROWS, width), jnp.bfloat16),
         name="send_blocks",
-    )(query_rows, cand)
+    )(me, query_rows, cand)
 
 
 def best_kernel(owner_shift, capacity, q_ref, cand_ref, cent_ref, best_ref, target_ref, qt_ref, acc_ref):
     step = pl.program_id(0)
-    rows = min(cent_ref.shape[0], 2048)
+    rows = min(cent_ref.shape[0], 4096)
 
     @pl.when(step == 0)
     def _():
@@ -114,10 +121,9 @@
 def score_kernel(
     sizes,
     me_ref,
-    cand_ref,
+    sent_ref,
     best_ref,
     levels_ref,
-    query_ref,
     cent_hbm,
     words_hbm,
     codes_hbm,
@@ -127,6 +133,7 @@
     table,
     words,
     query_t,
+    dense,
     embed,
     maxima,
     ids_vmem,
@@ -143,7 +150,8 @@
     small_sem,
 ):
     group_count, cent_count, per_device, query_len, capacity, pass_dev, cand_count = sizes
-    sources, pairs = cand_ref.shape
+    sources, sent_rows, pairs = sent_ref.shape
+    own_rows = sent_rows - DIGIT_ROWS
     items = sources * capacity
     tiles = words.shape[1] // SUB
     tile_tokens = SUB * FIELDS
@@ -175,8 +183,11 @@
     for part in range(word_parts):
         words_copy(part).start()
 
+    digits = sent_ref[:, own_rows:, :].astype(jnp.float32)
+    place = lax.broadcasted_iota(jnp.int32, digits.shape, 1)
+    scale = jnp.where(place < DIGITS, jnp.left_shift(1, 8 * jnp.minimum(place, DIGITS - 1)), 0)
     first = me_ref[0] * pass_dev
-    local = cand_ref[...] - first
+    local = jnp.sum(digits * scale.astype(jnp.float32), axis=1).astype(jnp.int32) - first
     mine = (local >= 0) & (local < pass_dev)
     earlier = lax.broadcasted_iota(jnp.int32, (pairs, pairs), 0) < lax.broadcasted_iota(
         jnp.int32, (pairs, pairs), 1
@@ -196,7 +207,6 @@
     ids_copy.start()
 
     maxima[...] = jnp.full(maxima.shape, MASKED, jnp.float32)
-    embed[...] = jnp.zeros(embed.shape, embed.dtype)
     lens_copy.wait()
     ids_copy.wait()
 
@@ -209,13 +219,12 @@
         table_copy(quad).wait()
         rows = pl.ds(pl.multiple_of(quad * part_rows, part_rows), part_rows)
         table[rows, :] = staged[rows, :].astype(jnp.float32)
-        block = query_ref[pl.ds(pl.multiple_of(quad * LANES, LANES), LANES), :]
-        query_t[quad] = jnp.transpose(block.astype(jnp.float32)).astype(jnp.bfloat16)
+        block = [sent_ref[quad * quad_sources + part, :own_rows, :] for part in range(quad_sources)]
+        block = jnp.concatenate(block, axis=0).astype(jnp.float32)
+        query_t[quad] = jnp.transpose(block).astype(jnp.bfloat16)
         start = count
-        group = quad // (cent_count // quad_sources)
-        cent = (quad % (cent_count // quad_sources)) * quad_sources
         for part in range(quad_sources):
-            source = (cent + part) * group_count + group
+            source = quad * quad_sources + part
             for slot in range(capacity):
                 tag = ids[source, slot] - 1
                 item = source * capacity + slot
@@ -237,11 +246,11 @@
         return count
 
     total = lax.fori_loop(0, quads, prepare, 0)
-    for index in range(BLOCKS):
+    for index in range(2 * BLOCKS):
         work[total + index] = spare
-    for index in range(BLOCKS // ALIGN):
+    for index in range(2 * BLOCKS // ALIGN):
         work_quad[total // ALIGN + index] = 0
-    chunks = (total + BLOCKS - 1) // BLOCKS
+    chunks = jnp.maximum((total + BLOCKS - 1) // BLOCKS, 2)
     codes_copy.wait()
     for part in range(word_parts):
         words_copy(part).wait()
@@ -271,9 +280,8 @@
             entry = work[chunk * BLOCKS + index]
             item, tile = jnp.right_shift(entry, tile_bits), jnp.bitwise_and(entry, tiles - 1)
             passage = item_pass[item]
+            start = passage * (tiles * tile_tokens) + tile * tile_tokens
             word = words[passage, pl.ds(pl.multiple_of(tile * SUB, SUB), SUB), :]
-            dense = []
-            start = passage * (tiles * tile_tokens) + tile * tile_tokens
             for field in range(FIELDS):
                 rows = jnp.zeros((SUB, LANES), jnp.float32)
                 for row in range(SUB):
@@ -284,22 +292,30 @@
                 residual = jnp.where(
                     high, jnp.where(low, level[3], level[2]), jnp.where(low, level[1], level[0])
                 )
-                dense.append(rows + residual)
-            dense = jnp.concatenate(dense, axis=0)
-            inverse = lax.rsqrt(jnp.sum(dense * dense, axis=1, keepdims=True) + 1e-06)
-            embed[index * tile_tokens : (index + 1) * tile_tokens, :] = (dense * inverse).astype(jnp.bfloat16)
-
-    @pl.when(chunks > 0)
-    def _():
-        decode(0)
-
-        def both(chunk, carry):
-            score(chunk - 1)
-            decode(chunk)
-            return carry
-
-        lax.fori_loop(1, chunks, both, 0)
-        score(chunks - 1)
+                base = index * tile_tokens + field * SUB
+                dense[base : base + SUB, :] = rows + residual
+
+    def normalize():
+        for index in range(BLOCKS):
+            rows = slice(index * tile_tokens, (index + 1) * tile_tokens)
+            block = dense[rows, :]
+            inverse = lax.rsqrt(jnp.sum(block * block, axis=1, keepdims=True) + 1e-06)
+            embed[rows, :] = (block * inverse).astype(jnp.bfloat16)
+
+    decode(0)
+    normalize()
+    decode(1)
+
+    def step(chunk, carry):
+        score(chunk - 2)
+        normalize()
+        decode(chunk)
+        return carry
+
+    lax.fori_loop(2, chunks, step, 0)
+    score(chunks - 2)
+    normalize()
+    score(chunks - 1)
 
     best = maxima[0, :items, :]
     for tile in range(1, tiles):
@@ -320,23 +336,23 @@
         out_ref[source, rows_best : rows_best + 1, :] = by_source[source : source + 1, :]
 
 
-def owner_scores(me, cand_all, best, query_all, centroids, token_codes, resid_words, lengths, levels, sizes):
+def owner_scores(me, sent, best, centroids, token_codes, resid_words, lengths, levels, sizes):
     capacity = sizes[4]
-    sources, pairs = cand_all.shape
+    sources, sent_rows, _ = sent.shape
     cent_dev, width = centroids.shape
     pass_dev, plen = token_codes.shape
     packed = resid_words.shape[1]
     tiles = packed // SUB
     items = sources * capacity
-    quads = query_all.shape[0] // LANES
-    work_size = items * tiles + quads * ALIGN + BLOCKS
+    quads = sources * (sent_rows - DIGIT_ROWS) // LANES
+    work_size = items * tiles + quads * ALIGN + 2 * BLOCKS
     reply_rows = (best.shape[0] + SUB) // SUB * SUB
     any_space = pl.BlockSpec(memory_space=pl.ANY)
     vmem = pl.BlockSpec(memory_space=pltpu.VMEM)
     tokens = items * plen
     return pl.pallas_call(
         functools.partial(score_kernel, sizes),
-        in_specs=[pl.BlockSpec(memory_space=pltpu.SMEM), vmem, vmem, vmem, vmem] + [any_space] * 4,
+        in_specs=[pl.BlockSpec(memory_space=pltpu.SMEM), vmem, vmem, vmem] + [any_space] * 4,
         out_specs=vmem,
         out_shape=jax.ShapeDtypeStruct((sources, reply_rows, LANES), jnp.float32),
         scratch_shapes=[
@@ -344,6 +360,7 @@
             pltpu.VMEM((cent_dev + SUB, width), jnp.float32),
             pltpu.VMEM((pass_dev, packed, width), jnp.int32),
             pltpu.VMEM((quads, width, LANES), jnp.bfloat16),
+            pltpu.VMEM((BLOCKS * SUB * FIELDS, width), jnp.float32),
             pltpu.VMEM((BLOCKS * SUB * FIELDS, width), jnp.bfloat16),
             pltpu.VMEM((tiles, items + SUB, LANES), jnp.float32),
             pltpu.VMEM((sources, LANES), jnp.int32),
@@ -364,7 +381,7 @@
             flops=2 * tokens * width * LANES, bytes_accessed=2 * cent_dev * width * 2, transcendentals=tokens
         ),
         name="owner_scores",
-    )(me, cand_all, best, levels, query_all, centroids, resid_words, token_codes.reshape(pass_dev * plen), lengths)
+    )(me, sent, best, levels, centroids, resid_words, token_codes.reshape(pass_dev * plen), lengths)
 
 
 def finish_kernel(sizes, me_ref, back_ref, target_ref, best_out, score_out):
@@ -419,13 +436,12 @@
     cand = candidates.reshape(per_device, cand_count)
     query_rows = queries.reshape(group_rows * query_len, width)
     me = (lax.axis_index("cent") * group_count + lax.axis_index("grp")).astype(jnp.int32).reshape(1)
-    ids_sent, rows_sent = send_blocks(query_rows, cand, devices, group_count)
-    cand_all = lax.all_to_all(ids_sent, ("cent", "grp"), split_axis=0, concat_axis=0, tiled=True)
-    query_all = lax.all_to_all(rows_sent, "grp", split_axis=0, concat_axis=0, tiled=True)
+    own_rows = per_device * query_len
+    sent = send_blocks(me, query_rows, cand, devices, own_rows, group_count)
+    sent = lax.all_to_all(sent, ("cent", "grp"), split_axis=0, concat_axis=0, tiled=True)
     best, target = centroid_best(query_rows, cand, centroids, pass_dev, capacity)
-    query_all = query_all.reshape(group_count * group_rows * query_len, width)
     reply = owner_scores(
-        me, cand_all, best, query_all, centroids, token_codes, resid_words, lengths, levels, sizes
+        me, sent, best, centroids, token_codes, resid_words, lengths, levels, sizes
     )
     back = lax.all_to_all(reply, ("cent", "grp"), split_axis=0, concat_axis=0, tiled=True)
     token_best, scores = finish(me, back, target, group_rows, sizes)

time: 84.5 us -> 75.5 us (0.89); the launches traced: 84.7 us -> 74.8 us
  Pallas kernels: 49.2 us -> 35.7 us
  blocking collectives: 16.1 us -> 24.6 us
  starting transfers between devices: 10.8 us -> 7.3 us
  waiting for transfers between devices: 7.14 us -> 5.77 us
    pallas_call x1, Pallas kernels: 32.1 us -> 19.8 us  [owner_scores(): pl.pallas_call(functools.partial(score_kernel, sizes), in_specs=[pl.Block...]
    all_to_all x1, blocking collectives: 16.1 us -> 24.6 us  [shards(): lax.all_to_all(reply, ('cent', 'grp'), split_axis=0, concat_axis=0, tiled...]
    all_to_all x2 -> x1, starting transfers between devices: 10.8 us -> 7.3 us  [shards(): lax.all_to_all(sent, ('cent', 'grp'), split_axis=0, concat_axis=0, tiled=...]
    all_to_all x2 -> x1, waiting for transfers between devices: 7.14 us -> 5.77 us  [shards(): lax.all_to_all(sent, ('cent', 'grp'), split_axis=0, concat_axis=0, tiled=...]
    pallas_call x1, Pallas kernels: 13.4 us -> 12.1 us  [centroid_best(): pl.pallas_call(functools.partial(best_kernel, pass_dev.bit_length() - 1,...]
  transfers between devices with their start and end apart: 2 -> 1, of which waited for: 1 -> 1; matrix products, arithmetic and copies ran while one was open for 0% -> 0% of each run, Pallas kernels for 16% -> 16%
where the time goes in v3:
time: 75.5 us; the launch traced here: 74.8 us
  Pallas kernels  35.7 us (47%)
  blocking collectives  24.6 us (33%)
  starting transfers between devices  7.3 us (10%)
  waiting for transfers between devices  5.77 us (8%)
  local copies, waits for them, and re-layouts  0.85 us (1%)
    all_to_all x1, blocking collectives, shards(): lax.all_to_all(reply, ('cent', 'grp'), split_axis=0, concat_axis=0, tiled...  24.6 us
    pallas_call x1, Pallas kernels, owner_scores(): pl.pallas_call(functools.partial(score_kernel, sizes), in_specs=[pl.Block...  19.8 us
    pallas_call x1, Pallas kernels, centroid_best(): pl.pallas_call(functools.partial(best_kernel, pass_dev.bit_length() - 1,...  12.1 us
    all_to_all x1, starting transfers between devices, shards(): lax.all_to_all(sent, ('cent', 'grp'), split_axis=0, concat_axis=0, tiled=...  7.3 us
    all_to_all x1, waiting for transfers between devices, shards(): lax.all_to_all(sent, ('cent', 'grp'), split_axis=0, concat_axis=0, tiled=...  5.77 us
    pallas_call x1, Pallas kernels, finish(): pl.pallas_call(functools.partial(finish_kernel, sizes), in_specs=[pl.Bloc...  1.92 us
    pallas_call x1, Pallas kernels, send_blocks(): pl.pallas_call(functools.partial(send_kernel, group_count.bit_length() -...  1.84 us
  transfers between devices with their start and end apart: 1, of which 1 were waited for; matrix products, arithmetic and copies ran while one was open for 0% of the time, Pallas kernels for 16%

profile of v3, /device:TPU:0, one launch (start us, length us, event | category | flops | bytes accessed | tf_op | source)
XLA Modules:
  0.0 74.8 jit_solution(7187456416654017211)
XLA Ops:
  0.6 1.8 %send_blocks.1 = bf16[32,80,128]{2,1,0:T(8,128)(2,1)} custom-call(s32[1]{0:T(128)} %bitcast.me_ref, bf16[512,128]{1,0:T(8,128)(2,1)} %bitcast.6, s32[2,64]{1,0:T(2,128)} %bitcast.8), custom_call_target="tpu_custom_call" | custom-call | tf_op jit(solution)/shard_map/send_blocks/pallas_call | solution.py:48
  2.5 7.3 %all-to-all-start = ((bf16[32,80,128]{2,1,0:T(8,128)(2,1)}), bf16[32,80,128]{2,1,0:T(8,128)(2,1)S(1)}, u32[]{:S(2)}, u32[]{:S(2)}) async-start(bf16[32,80,128]{2,1,0:T(8,128)(2,1)} %send_blocks.1), calls=%async_computation | async-start | bytes 1310720 | tf_op jit(solution)/shard_map/all_to_all | solution.py:441
  9.8 12.1 %centroid_best.1 = (f32[4,128]{1,0:T(4,128)}, s32[1,128]{1,0:T(1,128)}) custom-call(bf16[512,128]{1,0:T(8,128)(2,1)} %bitcast.7, s32[2,64]{1,0:T(2,128)} %bitcast.9, bf16[32768,128]{1,0:T(8,128)(2,1)} %cent_hbm.1), custom_call_target="tpu_custom_call" | custom-call | flops 4294967296 | bytes 8388608 | tf_op jit(solution)/shard_map/centroid_best/pallas_call | solution.py:93
  21.9 5.8 %all-to-all-done.sent_ref = bf16[32,80,128]{2,1,0:T(8,128)(2,1)S(1)} async-done(((bf16[32,80,128]{2,1,0:T(8,128)(2,1)}), bf16[32,80,128]{2,1,0:T(8,128)(2,1)S(1)}, u32[]{:S(2)}, u32[]{:S(2)}) %all-to-all-start) | async-done | bytes 655392 | tf_op jit(solution)/shard_map/all_to_all | solution.py:441
  27.7 0.0 copy-start
  27.7 0.8 %copy-done = bf16[32,80,128]{2,1,0:T(8,128)(2,1)} copy-done((bf16[32,80,128]{2,1,0:T(8,128)(2,1)}, bf16[32,80,128]{2,1,0:T(8,128)(2,1)S(1)}, u32[]{:S(2)}) %copy-start) | copy-done | bytes 655384
  28.5 19.8 %owner_scores.1 = f32[32,8,128]{2,1,0:T(8,128)} custom-call(s32[1]{0:T(128)} %bitcast.me_ref, bf16[32,80,128]{2,1,0:T(8,128)(2,1)} %copy-done, f32[4,128]{1,0:T(4,128)} %get-tuple-element.6.best_ref, f32[4,128]{1,0:T(4,128)} %levels_ref.1, bf16[32768,128]{1,0:T(8,128)(2,1)} %cent_hbm.1, s32[512,32,128]{2,1,0:T(8,128)} %words_hbm.1, s32[65536]{0:T(1024)} %bitcast.5, ...), custom_call_target="tpu_custom_call" | custom-call | flops 1073741824 | bytes 16777216 | tf_op jit(solution)/shard_map/owner_scores/pallas_call | solution.py:353
  48.3 24.6 %all_to_all.10.back_ref = f32[32,8,128]{2,1,0:T(8,128)} all-to-all(f32[32,8,128]{2,1,0:T(8,128)} %owner_scores.1), channel_id=1, replica_groups=mesh['cent'=8,'grp'=4] {'cent','grp'}, dimensions={0} | all-to-all | bytes 262144 | tf_op jit(solution)/shard_map/all_to_all | solution.py:446
  72.9 1.9 %finish.1 = (f32[16,32]{1,0:T(8,128)}, f32[2,64]{1,0:T(2,128)}) custom-call(s32[1]{0:T(128)} %bitcast.me_ref, f32[32,8,128]{2,1,0:T(8,128)} %all_to_all.10.back_ref, s32[1,128]{1,0:T(1,128)} %get-tuple-element.7.target_ref), custom_call_target="tpu_custom_call" | custom-call | tf_op jit(solution)/shard_map/finish/pallas_call | solution.py:414
Async XLA Ops:
  2.5 25.2 %all-to-all-start = ((bf16[32,80,128]{2,1,0:T(8,128)(2,1)}), bf16[32,80,128]{2,1,0:T(8,128)(2,1)S(1)}, u32[]{:S(2)}, u32[]{:S(2)}) async-start(bf16[32,80,128]{2,1,0:T(8,128)(2,1)} %send_blocks.1), calls=%async_computation | async-start | bytes 1310720 | tf_op jit(solution)/shard_map/all_to_all | solution.py:441
  27.7 0.8 %copy-start = (bf16[32,80,128]{2,1,0:T(8,128)(2,1)}, bf16[32,80,128]{2,1,0:T(8,128)(2,1)S(1)}, u32[]{:S(2)}) copy-start(bf16[32,80,128]{2,1,0:T(8,128)(2,1)S(1)} %all-to-all-done.sent_ref) | copy-start | bytes 1966084
